TPU v7x, 32 devices: a whole 2x2x4 slice. The times are simulated.
32 devices in a mesh: ctx: 32 (over z, y, x, core), exp: 1.
Axes of the slice: x: 2, y: 2, z: 4, core: 2. Of those that a mesh axis runs over, the one named last changes fastest.
Arguments:
- tokens: bfloat16 [4096, 2880], P('ctx', 'exp'), may hold values from -6 to 6
- route_ids: int32 [4096, 4], P('ctx'), may hold values from 0 to 31, all different within a row; in each aligned block of 128 rows (0 to 127, 128 to 255, ...) at most 20 rows name the same one
- combine: float32 [4096, 4], P('ctx'), may hold values from 0.05 to 0.6
- gain_attn: float32 [2880], replicated, may hold values from 0.25 to 1.75
- gain_moe: float32 [2880], replicated, may hold values from 0.25 to 1.75
- query_weight: bfloat16 [2880, 4096], P(None, ('exp', 'ctx'))
- key_weight: bfloat16 [2880, 512], P(None, ('exp', 'ctx')), may hold values from -0.109375 to 0.109375
- value_weight: bfloat16 [2880, 512], P(None, ('exp', 'ctx')), may hold values from -0.109375 to 0.109375
- attn_sinks: float32 [64], P('exp'), may hold values from 1 to 6
- out_weight: bfloat16 [4096, 2880], P('exp', 'ctx'), may hold values from -0.09375 to 0.09375
- gate_up_weight: bfloat16 [32, 2, 2880, 2880], P('ctx', None, None, 'exp'), may hold values from -0.109375 to 0.109375
- down_weight: bfloat16 [32, 2880, 2880], P('ctx', 'exp'), may hold values from -0.109375 to 0.109375
Outputs:
- layer_out: bfloat16 [4096, 2880], P('ctx', 'exp')
Inputs may be any that keep to these rules, and one draw needn't show every extreme that they name: `route_ids`: in each aligned block of 128 rows (the tokens of one index of ctx) no expert is named by more than 20 rows, a bound that some block reaches.
All inputs are finite; a program needn't handle non-finite values.
Results may differ from a plain program's by a relative error of at most 0.02.
Values may be sent and summed in bfloat16 or wider, within the bound.
No kernel may reach another device: no remote copies, remote signals or barrier semaphores. Data moves between devices by JAX's collectives and lax.ppermute only.
A program may use at most 256 MiB of HBM per device.

v0:
```python
import functools
import math

import jax
import jax.numpy as jnp
from jax import lax
from jax.experimental import pallas as pl
from jax.experimental.pallas import tpu as pltpu
from jax.sharding import PartitionSpec as P

HD = 64
WINDOW = 128
EPSILON = 1e-05
ROPE_BASE = 150000.0
PLANE = 8
BF16 = jnp.bfloat16
F32 = jnp.float32


def rms_norm(values, gain):
    wide = values.astype(F32)
    meansq = jnp.mean(wide * wide, axis=-1, keepdims=True)
    return (wide * lax.rsqrt(meansq + EPSILON) * gain).astype(BF16)


def rms_norm_t(values, gain):
    wide = values.astype(F32)
    meansq = jnp.mean(wide * wide, axis=0, keepdims=True)
    return (wide * lax.rsqrt(meansq + EPSILON) * gain[:, None]).astype(BF16)


def rotary(values, angles_pos):
    half_dim = values.shape[-1] // 2
    inverse_freq = jnp.exp(
        -(2.0 * jnp.arange(half_dim, dtype=F32) / values.shape[-1]) * math.log(ROPE_BASE)
    )
    angles = angles_pos[:, None] * inverse_freq[None, :]
    cosine = jnp.cos(angles)[:, None, :]
    sine_part = jnp.sin(angles)[:, None, :]
    first_half = values[..., :half_dim]
    second_half = values[..., half_dim:]
    return jnp.concatenate(
        [
            first_half * cosine - second_half * sine_part,
            second_half * cosine + first_half * sine_part,
        ],
        axis=-1,
    )


def sink_softmax(scores, key_mask, sink_col):
    masked = jnp.where(key_mask, scores, -1e30)
    row_top = jnp.maximum(jnp.max(masked, axis=-1, keepdims=True), sink_col)
    weights = jnp.where(key_mask, jnp.exp(masked - row_top), 0.0)
    denominator = jnp.sum(weights, axis=-1, keepdims=True) + jnp.exp(sink_col - row_top)
    return (weights / denominator).astype(BF16)


def attend_block(query_rows, key_rows, value_rows, query_pos, key_pos, sink_col):
    scores = jnp.einsum(
        "qkgd,skd->kgqs", query_rows, key_rows, preferred_element_type=F32
    ) * HD ** (-0.5)
    distance = query_pos[:, None] - key_pos[None, :]
    key_mask = (distance >= 0) & (distance < WINDOW) & (key_pos >= 0)[None, :]
    weights = sink_softmax(scores, key_mask, sink_col)
    mixed_rows = jnp.einsum("kgqs,skd->qkgd", weights, value_rows, preferred_element_type=F32)
    return mixed_rows.astype(BF16).reshape(query_rows.shape[0], -1)


def dot32(a, b):
    return jnp.dot(a, b, preferred_element_type=F32)


def project_whole(
    tokens, gain_attn, query_weight, key_weight, value_weight, attn_sinks, out_weight, early
):
    tok_dev = tokens.shape[0]
    full_rows = lax.all_gather(tokens, "exp", axis=1, tiled=True)
    normed = rms_norm(full_rows, gain_attn)
    pieces = lax.all_gather((query_weight, key_weight, value_weight), "ctx", axis=1, tiled=True)
    query_lin, key_lin, value_lin = tuple(dot32(normed, piece) for piece in pieces)
    heads_local = query_lin.shape[1] // HD
    kv_local = key_lin.shape[1] // HD
    group_size = heads_local // kv_local
    position_ids = lax.axis_index("ctx") * tok_dev + jnp.arange(tok_dev, dtype=jnp.int32)
    angles_pos = position_ids.astype(F32)
    query = rotary(query_lin.reshape(tok_dev, heads_local, HD), angles_pos).astype(BF16)
    keys_own = rotary(key_lin.reshape(tok_dev, kv_local, HD), angles_pos).astype(BF16)
    key_value = jnp.stack([keys_own.reshape(tok_dev, kv_local * HD), value_lin.astype(BF16)])
    n_ctx = lax.axis_size("ctx")
    previous = lax.ppermute(key_value, "ctx", [(i, i + 1) for i in range(n_ctx - 1)])
    context = jnp.concatenate([previous, key_value], axis=1)
    key_pos = position_ids[0] - WINDOW + jnp.arange(tok_dev + WINDOW, dtype=jnp.int32)
    attended = attend_block(
        query.reshape(tok_dev, kv_local, group_size, HD),
        context[0].reshape(-1, kv_local, HD),
        context[1].reshape(-1, kv_local, HD),
        position_ids,
        key_pos,
        attn_sinks.reshape(kv_local, group_size, 1, 1),
    )
    head_terms = dot32(attended, lax.all_gather(out_weight, "ctx", axis=1, tiled=True))
    attn_proj = lax.psum(head_terms.astype(BF16), "exp").astype(F32)
    return (full_rows.astype(F32) + attn_proj).astype(BF16).T, early


def dot_nt(a, b):
    return lax.dot_general(a, b, (((1,), (1,)), ((), ())), preferred_element_type=F32)


def turn(values, cosine, signed_sine):
    width = values.shape[1]
    half = HD // 2
    lane = lax.broadcasted_iota(jnp.int32, values.shape, 1) % HD
    partner = jnp.where(
        lane < half,
        pltpu.roll(values, width - half, 1),
        pltpu.roll(values, half, 1),
    )
    return values * cosine + partner * signed_sine


def qkv_kernel(count, place_ref, *refs):
    blocks, shares, refs = refs[:count], refs[count : count + PLANE], refs[count + PLANE :]
    cos_ref, sin_ref, q_ref, key_value_ref, rows_ref, kv_ref = refs
    width, rows = blocks[0].shape
    cols = shares[0].shape[1]
    share = kv_ref.shape[2]
    for r in range(count):
        rows_ref[r * rows : (r + 1) * rows, :] = blocks[r][...].T

    for i in range(PLANE):
        for tile in range(-(-width // cols)):
            at, lanes = width + 2 * share * tile, slice(tile * cols, (tile + 1) * cols)
            for part in range(2):
                kv_ref[part, place_ref[i], :, lanes] = shares[i][at + part * share : at + (part + 1) * share]
    both = kv_ref[...].reshape(2 * PLANE * share, kv_ref.shape[3])[:, :width]
    lines = dot_nt(rows_ref[...], both)
    half = PLANE * share
    for r in range(count):
        piece = lines[r * rows : (r + 1) * rows]
        key_value_ref[r, :, :half] = turn(piece[:, :half], cos_ref[r], sin_ref[r]).astype(BF16)
        key_value_ref[r, :, half:] = piece[:, half:].astype(BF16)

    for i in range(0, PLANE, 2):
        weight = jnp.concatenate([shares[i][:width], shares[i + 1][:width]], axis=1)
        query = dot32(rows_ref[...], weight)
        for k in range(2):
            lanes = pl.ds(pl.multiple_of(place_ref[i + k] * cols, cols), cols)
            for r in range(count):
                piece = query[r * rows : (r + 1) * rows, k * cols : (k + 1) * cols]
                q_ref[r, :, lanes] = turn(piece, cos_ref[r], sin_ref[r]).astype(BF16)


def project_blocks(place, blocks, shares, share, cosine, signed_sine):
    count = len(blocks)
    width, rows = blocks[0].shape
    cols = shares[0].shape[1]
    tiles = -(-width // cols)
    kv_cols = 2 * PLANE * share
    vmem = pl.BlockSpec(memory_space=pltpu.VMEM)
    return pl.pallas_call(
        functools.partial(qkv_kernel, count),
        in_specs=[pl.BlockSpec(memory_space=pltpu.SMEM)] + [vmem] * (count + PLANE + 2),
        out_specs=[vmem, vmem],
        out_shape=[
            jax.ShapeDtypeStruct((count, rows, PLANE * cols), BF16),
            jax.ShapeDtypeStruct((count, rows, kv_cols), BF16),
        ],
        scratch_shapes=[
            pltpu.VMEM((count * rows, width), BF16),
            pltpu.VMEM((2, PLANE, share, tiles * cols), BF16),
        ],
        compiler_params=pltpu.CompilerParams(vmem_limit_bytes=40 * 2**20),
        cost_estimate=pl.CostEstimate(
            flops=2 * count * rows * width * (PLANE * cols + kv_cols),
            bytes_accessed=2 * width * (PLANE * cols + kv_cols + count * rows),
            transcendentals=0,
        ),
    )(place, *blocks, *shares, cosine, signed_sine)


def attend_kernel(
    numbers, place_ref, sinks_ref, queries_ref, key_values_ref, halos_ref, weight_hbm, out_ref, att_ref, weight_ref, copied
):
    copy = pltpu.make_async_copy(weight_hbm, weight_ref, copied)
    copy.start()
    count, rows = key_values_ref.shape[:2]
    pair = 2 * HD
    kv_heads = key_values_ref.shape[2] // pair
    kv_cols = kv_heads * HD
    pairs = queries_ref.shape[2] // pair
    lane = lax.broadcasted_iota(jnp.int32, (rows, pair), 1)
    low = lane < HD

    def spread(values, head):
        moved = pltpu.roll(values.astype(F32), HD, 1)
        chunk = values.astype(F32)
        lower, upper = (chunk, moved) if head % 2 == 0 else (moved, chunk)
        zero = jnp.zeros_like(chunk)
        return jnp.concatenate(
            [jnp.where(low, lower, zero), jnp.where(low, zero, upper)], axis=0
        ).astype(BF16)

    def side(ref):
        tables = []
        for head in range(kv_heads):
            at = head // 2 * pair
            keys = spread(ref[:, at : at + pair], head)
            values = spread(ref[:, kv_cols + at : kv_cols + at + pair], head)
            tables.append((keys, values))
        return tables

    row = lax.broadcasted_iota(jnp.int32, (rows, rows), 0)
    col = lax.broadcasted_iota(jnp.int32, (rows, rows), 1)
    inside = col <= row
    scale = HD**-0.5
    for i, r in enumerate(numbers):
        own, previous = side(key_values_ref.at[r]), side(halos_ref.at[place_ref[count + r]])
        shown = jnp.logical_or(inside, place_ref[r] == 0)
        for p in range(pairs):
            head = p * kv_heads // pairs
            chunk = queries_ref[r, :, p * pair : (p + 1) * pair]
            scores_own = dot_nt(chunk, own[head][0])
            scores_previous = dot_nt(chunk, previous[head][0])
            probs_own, probs_previous = [], []
            for h in range(2):
                half = slice(h * rows, (h + 1) * rows)
                scores = jnp.where(inside, scores_own[:, half], scores_previous[:, half]) * scale
                scores = jnp.where(shown, scores, -1e30)
                sink = sinks_ref[2 * p + h]
                top = jnp.maximum(jnp.max(scores, axis=1, keepdims=True), sink)
                weights = jnp.exp(scores - top)
                total = jnp.sum(weights, axis=1, keepdims=True) + jnp.exp(sink - top)
                probs = weights / total
                probs_own.append(jnp.where(inside, probs, 0.0).astype(BF16))
                probs_previous.append(jnp.where(inside, 0.0, probs).astype(BF16))
            mixed = dot32(jnp.concatenate(probs_own, axis=1), own[head][1])
            mixed = mixed + dot32(jnp.concatenate(probs_previous, axis=1), previous[head][1])
            att_ref[i * rows : (i + 1) * rows, p * pair : (p + 1) * pair] = mixed.astype(BF16)

    shares, groups, padded, depth = weight_ref.shape
    cols = out_ref.shape[1] // (shares * groups)
    attended = att_ref[...]
    copy.wait()
    for p in range(shares):
        terms = dot_nt(weight_ref[p].reshape(groups * padded, depth), attended)
        for g in range(groups):
            at = (g * shares + p) * cols
            for i in range(len(numbers)):
                out_ref[i, at : at + cols, :] = terms[g * padded : g * padded + cols, i * rows : (i + 1) * rows]


def attend_and_project(numbers, place, sinks, queries, key_values, halos, weight, width):
    rows = queries.shape[1]
    count = len(numbers)
    depth = weight.shape[3]
    vmem = pl.BlockSpec(memory_space=pltpu.VMEM)
    smem = pl.BlockSpec(memory_space=pltpu.SMEM)
    return pl.pallas_call(
        functools.partial(attend_kernel, numbers),
        in_specs=[smem, smem] + [vmem] * 3 + [pl.BlockSpec(memory_space=pl.ANY)],
        out_specs=vmem,
        out_shape=jax.ShapeDtypeStruct((count, width, rows), F32),
        scratch_shapes=[
            pltpu.VMEM((count * rows, depth), BF16),
            pltpu.VMEM(weight.shape, BF16),
            pltpu.SemaphoreType.DMA,
        ],
        compiler_params=pltpu.CompilerParams(vmem_limit_bytes=56 * 2**20),
        cost_estimate=pl.CostEstimate(
            flops=2 * count * rows * depth * (width + 8 * rows),
            bytes_accessed=2 * width * (depth + 2 * count * rows),
            transcendentals=count * rows * rows * depth // HD,
        ),
    )(place, sinks, queries, key_values, halos, weight)


def project_planes(
    tokens, gain_attn, query_weight, key_weight, value_weight, attn_sinks, out_weight, early
):
    tok_dev, width = tokens.shape
    n_ctx = lax.axis_size("ctx")
    n_z = n_ctx // PLANE
    index = lax.axis_index("ctx")
    z, j = index // PLANE, index % PLANE
    planes = [[PLANE * a + b for b in range(PLANE)] for a in range(n_z)]
    order = list(range(0, n_z, 2)) + list(range(1, n_z, 2))[::-1]
    place_of = [order.index(a) for a in range(n_z)]
    ring, places = jnp.array(order, jnp.int32), jnp.array(place_of, jnp.int32)

    def shift(block, steps):
        return lax.ppermute(block, "ctx", [(i, (i + steps * PLANE) % n_ctx) for i in range(n_ctx)])

    def pass_on(block):
        route = [
            (a * PLANE + b, order[place_of[a] - 1] * PLANE + b) for a in range(n_z) for b in range(PLANE)
        ]
        return lax.ppermute(block, "ctx", route)

    def behind(block):
        route = [(a * PLANE + b, a * PLANE + (b + 1) % PLANE) for a in range(n_z) for b in range(PLANE)]
        return lax.ppermute(block, "ctx", route)

    def swap(block, bits):
        return lax.ppermute(block, "ctx", [(i, i ^ bits) for i in range(n_ctx)])

    tokens_t = tokens.T
    blocks = [rms_norm_t(tokens_t, gain_attn)]

    lanes = query_weight.shape[1]
    share = key_weight.shape[1]
    tiles = -(-width // lanes)
    kv_rows = jnp.concatenate([key_weight.T, value_weight.T], axis=0)
    kv_rows = jnp.pad(kv_rows, ((0, 0), (0, tiles * lanes - width))).reshape(2 * share, tiles, lanes)
    packed = jnp.concatenate(
        [query_weight, kv_rows.transpose(1, 0, 2).reshape(tiles * 2 * share, lanes)], axis=0
    )
    near, far = swap(packed, 2), swap(packed, 4)

    cols = out_weight.shape[1]
    padded = -(-cols // 16) * 16
    group_rows = out_weight.shape[0] // n_z
    out_rows = jnp.pad(out_weight.T, ((0, padded - cols), (0, 0)))
    out_rows, blocks[0] = lax.optimization_barrier((out_rows, blocks[0]))
    blocks.append(pass_on(blocks[0]))
    out_groups = jnp.stack(jnp.split(out_rows, n_z, axis=1))
    pieces = [
        shift(lax.dynamic_index_in_dim(out_groups, (z + s) % n_z, 0, keepdims=False), s) if s
        else lax.dynamic_index_in_dim(out_groups, z, 0, keepdims=False)
        for s in range(n_z)
    ]
    ordered = jnp.stack(pieces[::-1] + pieces[:0:-1])
    out_mine = lax.dynamic_slice_in_dim(ordered, n_z - 1 - z, n_z, 0)
    heads = PLANE * query_weight.shape[1] // HD
    sinks = lax.dynamic_slice_in_dim(attn_sinks, z * heads, heads)
    own_rows = jnp.arange(tok_dev, dtype=jnp.int32)
    lane = jnp.arange(2 * HD, dtype=jnp.int32) % HD
    half = HD // 2
    inverse_freq = jnp.exp(-(2.0 * (lane % half).astype(F32) / HD) * math.log(ROPE_BASE))
    mine = places[z]
    block_z = ring[(mine + jnp.arange(n_z, dtype=jnp.int32)) % n_z]
    numbers = block_z * PLANE + j
    angles = (numbers[:, None] * tok_dev + own_rows[None, :]).astype(F32)[:, :, None] * inverse_freq
    signed_sine = jnp.where(lane < half, -jnp.sin(angles), jnp.sin(angles))
    cosine = jnp.cos(angles)
    below = (places[jnp.maximum(block_z - 1, 0)] - mine) % n_z
    previous_at = jnp.where(j == 0, below, jnp.arange(n_z, dtype=jnp.int32))
    relative = jnp.arange(PLANE, dtype=jnp.int32) ^ j
    place = jnp.concatenate([(numbers == 0).astype(jnp.int32), previous_at])
    out_mine, near = lax.optimization_barrier((out_mine, near))
    out_all = lax.all_gather(out_mine, "ctx", axis_index_groups=planes)
    for _ in range(n_z - 2):
        blocks.append(pass_on(blocks[-1]))
    packed, blocks[1] = lax.optimization_barrier((packed, blocks[1]))
    corner = swap(packed, 6)
    second = min(2, n_z - 1)
    (near, far, blocks[second], cosine, signed_sine, place, relative, sinks, early) = lax.optimization_barrier(
        (near, far, blocks[second], cosine, signed_sine, place, relative, sinks, early)
    )
    shares = [packed, swap(packed, 1), near, swap(near, 1), far, swap(far, 1)]
    corner, blocks[-1] = lax.optimization_barrier((corner, blocks[-1]))
    shares += [corner, swap(corner, 1)]
    queries, key_values = project_blocks(relative, blocks, shares, share, cosine, signed_sine)
    halos = behind(key_values)

    def parts_of(numbers):
        return attend_and_project(numbers, place, sinks, queries, key_values, halos, out_all, width)

    running = parts_of((1,))[0].astype(BF16)
    others = parts_of(tuple(range(2, n_z)) + (0,))
    for i in range(n_z - 2):
        running = (pass_on(running).astype(F32) + others[i]).astype(BF16)
    total = pass_on(running).astype(F32) + others[n_z - 2]
    return (tokens_t.astype(F32) + total).astype(BF16), early


def expert_kernel(tile, hidden, rows_ref, gate_ref, upper_ref, down_ref, out_ref, total_ref):
    step = pl.program_id(0)
    steps = pl.num_programs(0)

    def add(count, initial):
        rows = rows_ref[...]
        gate = dot32(rows, gate_ref[0, :, :count])
        upper = dot32(rows, upper_ref[0, :, :count])
        activation = (gate * jax.nn.sigmoid(1.702 * gate) * (upper + 1.0)).astype(BF16)
        terms = dot32(activation, down_ref[:count, :])
        total_ref[...] = terms if initial else total_ref[...] + terms

    last = hidden - (-(-hidden // tile) - 1) * tile

    @pl.when(step == 0)
    def _():
        add(tile, True)

    @pl.when(jnp.logical_and(step > 0, step < steps - 1))
    def _():
        add(tile, False)

    @pl.when(step == steps - 1)
    def _():
        add(last, False)
        out_ref[...] = total_ref[...].astype(BF16)


def run_expert(rows, gate_up, down):
    count, width = rows.shape
    hidden = down.shape[0]
    tile = 512 if hidden > 1024 else 256
    return pl.pallas_call(
        functools.partial(expert_kernel, tile, hidden),
        grid=(-(-hidden // tile),),
        in_specs=[
            pl.BlockSpec((count, width), lambda f: (0, 0)),
            pl.BlockSpec((1, width, tile), lambda f: (0, 0, f)),
            pl.BlockSpec((1, width, tile), lambda f: (1, 0, f)),
            pl.BlockSpec((tile, width), lambda f: (f, 0)),
        ],
        out_specs=pl.BlockSpec((count, width), lambda f: (0, 0)),
        out_shape=jax.ShapeDtypeStruct((count, width), BF16),
        scratch_shapes=[pltpu.VMEM((count, width), F32)],
        compiler_params=pltpu.CompilerParams(vmem_limit_bytes=52 * 2**20),
        cost_estimate=pl.CostEstimate(
            flops=6 * count * width * hidden,
            bytes_accessed=6 * width * hidden + 4 * count * width,
            transcendentals=count * hidden,
        ),
    )(rows, gate_up, gate_up, down)


def slot_chunks(capacity):
    return [capacity - 8, 8] if capacity > 8 else [capacity]


def dispatch_kernel(chosen_ref, normed_ref, out_ref):
    out_ref[...] = dot_nt(chosen_ref[...], normed_ref[...]).astype(BF16)


def dispatch(chosen, normed):
    total, rows = chosen.shape
    width = normed.shape[0]
    return pl.pallas_call(
        dispatch_kernel,
        out_shape=jax.ShapeDtypeStruct((total, width), BF16),
        compiler_params=pltpu.CompilerParams(vmem_limit_bytes=24 * 2**20),
        cost_estimate=pl.CostEstimate(
            flops=2 * total * rows * width, bytes_accessed=2 * width * (total + rows), transcendentals=0
        ),
    )(chosen, normed)


def routing(route_ids, combine, n_ctx, sizes):
    tok_dev = route_ids.shape[0]
    named = route_ids[:, :, None] == jnp.arange(n_ctx, dtype=jnp.int32)[None, None, :]
    member = jnp.any(named, axis=1)
    weight_of = jnp.sum(jnp.where(named, combine[:, :, None], 0.0), axis=1)
    rows = jnp.arange(tok_dev, dtype=jnp.int32)
    earlier = (rows[:, None] > rows[None, :]).astype(BF16)
    slot_of = jnp.where(member, dot32(earlier, member.astype(BF16)), -1.0).T.astype(BF16)
    weight_of = weight_of.T
    high = weight_of.astype(BF16)
    low = (weight_of - high.astype(F32)).astype(BF16)
    table = jnp.concatenate([slot_of, high, low], axis=1)
    chunks = []
    first = 0
    for size in sizes:
        number = jnp.arange(n_ctx * size, dtype=jnp.int32)[:, None]
        device = (number // size == jnp.arange(n_ctx, dtype=jnp.int32)[None, :]).astype(BF16)
        spread = dot32(device, table)
        chosen = spread[:, :tok_dev] == (first + number % size).astype(F32)
        scale = jnp.where(jnp.concatenate([chosen, chosen], axis=1), spread[:, tok_dev:], 0.0).astype(BF16)
        chunks.append((chosen.astype(BF16), scale))
        first += size
    return chunks


def mix_experts(normed, sizes, matrices, gate_up, down):
    width, tok_dev = normed.shape
    n_ctx, n_exp = lax.axis_size("ctx"), lax.axis_size("exp")
    width_local = width // n_exp

    def tiles(rows, size):
        if size % 8 == 0 or size % 4:
            return rows.reshape(n_ctx, size, -1)
        return rows.reshape(n_ctx, size // 4, 4, -1)

    def exchange(parts):
        return lax.all_to_all(parts, "ctx", split_axis=0, concat_axis=0, tiled=True)

    def in_order(parts, earlier):
        return lax.optimization_barrier((parts, earlier))

    outgoing, received = [], []
    for size, (chosen, _) in zip(sizes, matrices):
        if outgoing:
            chosen, outgoing[-1] = in_order(chosen, outgoing[-1])
        outgoing.append(tiles(dispatch(chosen, normed), size))
    for parts in outgoing:
        if received:
            parts, received[-1] = in_order(parts, received[-1])
        received.append(exchange(parts))

    results = []
    for i, size in enumerate(sizes):
        if i > 1 and i == len(sizes) - 1:
            received[i], results[0] = in_order(received[i], results[0])
        if results:
            received[i], results[-1] = in_order(received[i], results[-1])
        rows_in = received[i].reshape(n_ctx * size, width)
        results.append(tiles(run_expert(rows_in, gate_up, down), size))

    answers = []
    for parts in results:
        if answers:
            parts, answers[-1] = in_order(parts, answers[-1])
        answers.append(exchange(parts))

    moe_out = jnp.zeros((width_local, tok_dev), F32)
    for size, (_, scale), answer in zip(sizes, matrices, answers):
        if n_exp > 1:
            answer = lax.psum_scatter(answer, "exp", scatter_dimension=answer.ndim - 1, tiled=True)
        terms = lax.dot_general(
            answer.reshape(n_ctx * size, width_local), scale, (((0,), (0,)), ((), ())),
            preferred_element_type=F32,
        )
        moe_out = moe_out + terms[:, :tok_dev] + terms[:, tok_dev:]
    return moe_out


def per_device(
    tokens,
    route_ids,
    combine,
    gain_attn,
    gain_moe,
    query_weight,
    key_weight,
    value_weight,
    attn_sinks,
    out_weight,
    gate_up_weight,
    down_weight,
):
    tok_dev, width_local = tokens.shape
    n_ctx = lax.axis_size("ctx")
    n_exp = lax.axis_size("exp")
    capacity = tok_dev * route_ids.shape[1] * 5 // (4 * n_ctx)
    sizes = slot_chunks(capacity)
    matrices = routing(route_ids, combine, n_ctx, sizes)
    by_planes = n_exp == 1 and n_ctx % PLANE == 0 and n_ctx > PLANE
    project = project_planes if by_planes else project_whole
    residual, matrices = project(
        tokens, gain_attn, query_weight, key_weight, value_weight, attn_sinks, out_weight, matrices
    )
    width = residual.shape[0]
    normed_moe = rms_norm_t(residual, gain_moe)
    exp_index = lax.axis_index("exp")
    residual_local = lax.dynamic_slice_in_dim(residual, exp_index * width_local, width_local, 0)

    moe_out = mix_experts(normed_moe, sizes, matrices, gate_up_weight[0], down_weight[0])
    return (residual_local.astype(F32) + moe_out).astype(BF16).T


def solution(mesh):
    return jax.shard_map(
        per_device,
        mesh=mesh,
        in_specs=(
            P("ctx", "exp"),
            P("ctx", None),
            P("ctx", None),
            P(),
            P(),
            P(None, ("exp", "ctx")),
            P(None, ("exp", "ctx")),
            P(None, ("exp", "ctx")),
            P("exp"),
            P("exp", "ctx"),
            P("ctx", None, None, "exp"),
            P("ctx", "exp", None),
        ),
        out_specs=P("ctx", "exp"),
        check_vma=False,
    )
```

profile of v0, /device:TPU:0, one launch (start us, length us, event | category | flops | bytes accessed | tf_op | source)
XLA Modules:
  0.0 395.9 jit_solution(17522231775891747527)
XLA Ops:
  10.9 5.0 %collective-permute-start = (bf16[96,1024]{1,0:T(8,128)(2,1)}, bf16[96,1024]{1,0:T(8,128)(2,1)}, u32[]{:S(2)}, u32[]{:S(2)}) collective-permute-start(bf16[96,1024]{1,0:T(8,128)(2,1)} %get-tuple-element.73), channel_id=1, source_target_pairs={{0,24},{1,25},{2,26},{3,27},{4,28},{5,29},{6,30},{7,31},{8,0},{9,1... | collective-permute-start | bytes 589832 | tf_op jit(solution)/shard_map/ppermute | solution.py:293
  18.8 2.8 collective-permute-done
  22.5 10.4 %collective-permute-done.1 = bf16[96,1024]{1,0:T(8,128)(2,1)} collective-permute-done((bf16[96,1024]{1,0:T(8,128)(2,1)}, bf16[96,1024]{1,0:T(8,128)(2,1)}, u32[]{:S(2)}, u32[]{:S(2)}) %collective-permute-start.1) | collective-permute-done | bytes 196640 | tf_op jit(solution)/shard_map/ppermute | solution.py:293
  40.4 2.5 collective-permute-start.5
  46.7 11.9 %collective-permute-done.5.refs_1_ = bf16[2880,128]{1,0:T(8,128)(2,1)} collective-permute-done((bf16[2880,128]{1,0:T(8,128)(2,1)S(1)}, bf16[2880,128]{1,0:T(8,128)(2,1)}, u32[]{:S(2)}, u32[]{:S(2)}) %collective-permute-start.5) | collective-permute-done | bytes 737312 | tf_op jit(solution)/shard_map/ppermute | solution.py:299
  61.6 14.6 %collective-permute-done.6.refs_2_ = bf16[2880,128]{1,0:T(8,128)(2,1)} collective-permute-done((bf16[2880,128]{1,0:T(8,128)(2,1)}, bf16[2880,128]{1,0:T(8,128)(2,1)}, u32[]{:S(2)}, u32[]{:S(2)}) %collective-permute-start.6) | collective-permute-done | bytes 737312 | tf_op jit(solution)/shard_map/ppermute | solution.py:299
  80.3 8.5 %collective-permute-done.4.refs_8_ = bf16[3616,128]{1,0:T(8,128)(2,1)} collective-permute-done((bf16[3616,128]{1,0:T(8,128)(2,1)S(1)}, bf16[3616,128]{1,0:T(8,128)(2,1)}, u32[]{:S(2)}, u32[]{:S(2)}) %collective-permute-start.4) | collective-permute-done | bytes 925728 | tf_op jit(solution)/shard_map/ppermute | solution.py:306
  89.3 3.6 collective-permute-done.8.refs_3_
  92.9 3.5 collective-permute-done.12.refs_11_
  96.4 7.3 %shard_map.136 = (bf16[4,128,1024]{2,1,0:T(8,128)(2,1)S(1)}, bf16[4,128,256]{2,1,0:T(8,128)(2,1)S(1)}) custom-call(s32[8]{0:T(128)S(1)} %get-tuple-element.40.place_ref, bf16[2880,128]{1,0:T(8,128)(2,1)S(1)} %fusion.15.refs_0_, bf16[2880,128]{1,0:T(8,128)(2,1)} %collective-permute-done.5.refs_1_, bf16[2880,128]{1,0:T(8,128)(2,1)} %collective-permute-done.6.refs_2_, ...), custom_call_target="tpu_custom_call" | custom-call | flops 3774873600 | bytes 10321920 | tf_op jit(solution)/shard_map/pallas_call | solution.py:162
  105.0 9.8 %collective-permute-done.13.halos_ref = bf16[4,128,256]{2,1,0:T(8,128)(2,1)S(1)} collective-permute-done((bf16[4,128,256]{2,1,0:T(8,128)(2,1)S(1)}, bf16[4,128,256]{2,1,0:T(8,128)(2,1)S(1)}, u32[]{:S(2)}, u32[]{:S(2)}) %collective-permute-start.13) | collective-permute-done | bytes 262176 | tf_op jit(solution)/shard_map/ppermute | solution.py:303
  115.5 7.3 %shard_map.137 = f32[1,2880,128]{2,1,0:T(8,128)} custom-call(s32[8]{0:T(128)} %get-tuple-element.38.place_ref, f32[16]{0:T(128)} %dynamic_slice.29.sinks_ref, bf16[4,128,1024]{2,1,0:T(8,128)(2,1)} %copy-done, bf16[4,128,256]{2,1,0:T(8,128)(2,1)} %copy-done.1, bf16[4,128,256]{2,1,0:T(8,128)(2,1)} %copy-done.9, bf16[8,4,96,1024]{3,2,1,0:T(8,128)(2,1)} %bitcast.95), custom_call_target="tpu_custom_call" | custom-call | flops 1023410176 | bytes 7372800 | tf_op jit(solution)/shard_map/pallas_call | solution.py:260
  125.8 15.5 %shard_map.138 = f32[3,2880,128]{2,1,0:T(8,128)} custom-call(s32[8]{0:T(128)} %get-tuple-element.38.place_ref, f32[16]{0:T(128)} %dynamic_slice.29.sinks_ref, bf16[4,128,1024]{2,1,0:T(8,128)(2,1)} %copy-done, bf16[4,128,256]{2,1,0:T(8,128)(2,1)} %copy-done.1, bf16[4,128,256]{2,1,0:T(8,128)(2,1)} %copy-done.9, bf16[8,4,96,1024]{3,2,1,0:T(8,128)(2,1)} %bitcast.96), custom_call_target="tpu_custom_call" | custom-call | flops 3070230528 | bytes 10321920 | tf_op jit(solution)/shard_map/pallas_call | solution.py:260
  141.3 2.3 collective-permute-done.14
  146.2 17.4 %collective-permute-done.15 = bf16[2880,128]{1,0:T(8,128)(2,1)S(1)} collective-permute-done((bf16[2880,128]{1,0:T(8,128)(2,1)S(1)}, bf16[2880,128]{1,0:T(8,128)(2,1)S(1)}, u32[]{:S(2)}, u32[]{:S(2)}) %collective-permute-start.15) | collective-permute-done | bytes 737312 | tf_op jit(solution)/shard_map/ppermute | solution.py:299
  166.6 16.3 %collective-permute-done.16 = bf16[2880,128]{1,0:T(8,128)(2,1)S(1)} collective-permute-done((bf16[2880,128]{1,0:T(8,128)(2,1)S(1)}, bf16[2880,128]{1,0:T(8,128)(2,1)S(1)}, u32[]{:S(2)}, u32[]{:S(2)}) %collective-permute-start.16) | collective-permute-done | bytes 737312 | tf_op jit(solution)/shard_map/ppermute | solution.py:299
  182.8 1.8 fusion.2
  186.7 2.1 reshape.261
  188.8 5.4 %all-to-all-start = ((bf16[32,3,4,2880]{3,2,1,0:T(4,128)(2,1)}), bf16[32,3,4,2880]{3,2,1,0:T(4,128)(2,1)S(1)}, u32[]{:S(2)}, u32[]{:S(2)}) async-start(bf16[32,3,4,2880]{3,2,1,0:T(4,128)(2,1)} %reshape.261), calls=%async_computation | async-start | bytes 4521984 | tf_op jit(solution)/shard_map/all_to_all | solution.py:488
  195.9 50.7 %all-to-all-done = bf16[32,3,4,2880]{3,2,1,0:T(4,128)(2,1)S(1)} async-done(((bf16[32,3,4,2880]{3,2,1,0:T(4,128)(2,1)}), bf16[32,3,4,2880]{3,2,1,0:T(4,128)(2,1)S(1)}, u32[]{:S(2)}, u32[]{:S(2)}) %all-to-all-start) | async-done | bytes 2211872 | tf_op jit(solution)/shard_map/all_to_all | solution.py:488
  246.6 4.1 %all-to-all-start.1 = ((bf16[32,8,2880]{2,1,0:T(8,128)(2,1)}), bf16[32,8,2880]{2,1,0:T(8,128)(2,1)}, u32[]{:S(2)}, u32[]{:S(2)}) async-start(bf16[32,8,2880]{2,1,0:T(8,128)(2,1)} %bitcast.25), calls=%async_computation.1 | async-start | bytes 3014656 | tf_op jit(solution)/shard_map/all_to_all | solution.py:488
  250.8 2.5 reshape.263.rows_ref
  253.2 29.2 %shard_map.141 = bf16[384,2880]{1,0:T(8,128)(2,1)} custom-call(bf16[384,2880]{1,0:T(8,128)(2,1)} %reshape.263.rows_ref, bf16[2,2880,2880]{2,1,0:T(8,128)(2,1)} %bitcast.89, bf16[2,2880,2880]{2,1,0:T(8,128)(2,1)} %bitcast.90, bf16[2880,2880]{1,0:T(8,128)(2,1)} %bitcast.93), custom_call_target="tpu_custom_call" | custom-call | flops 19110297600 | bytes 54190080 | tf_op jit(solution)/shard_map/pallas_call | solution.py:410
  282.4 4.0 %reshape.264 = bf16[32,3,4,2880]{3,2,1,0:T(4,128)(2,1)} reshape(bf16[384,2880]{1,0:T(8,128)(2,1)} %shard_map.141) | data formatting | bytes 4423680 | tf_op jit(solution)/shard_map/reshape | solution.py:485
  287.1 5.3 %all-to-all-start.2 = ((bf16[32,3,4,2880]{3,2,1,0:T(4,128)(2,1)}), bf16[32,3,4,2880]{3,2,1,0:T(4,128)(2,1)S(1)}, u32[]{:S(2)}, u32[]{:S(2)}) async-start(bf16[32,3,4,2880]{3,2,1,0:T(4,128)(2,1)} %reshape.264), calls=%async_computation.2 | async-start | bytes 4521984 | tf_op jit(solution)/shard_map/all_to_all | solution.py:488
  292.5 23.4 %shard_map.142 = bf16[256,2880]{1,0:T(8,128)(2,1)} custom-call(bf16[256,2880]{1,0:T(8,128)(2,1)} %bitcast.28.rows_ref, bf16[2,2880,2880]{2,1,0:T(8,128)(2,1)} %bitcast.91, bf16[2,2880,2880]{2,1,0:T(8,128)(2,1)} %bitcast.92, bf16[2880,2880]{1,0:T(8,128)(2,1)} %bitcast.94), custom_call_target="tpu_custom_call" | custom-call | flops 12740198400 | bytes 52715520 | tf_op jit(solution)/shard_map/pallas_call | solution.py:410
  315.9 29.0 %all-to-all-done.2 = bf16[32,3,4,2880]{3,2,1,0:T(4,128)(2,1)S(1)} async-done(((bf16[32,3,4,2880]{3,2,1,0:T(4,128)(2,1)}), bf16[32,3,4,2880]{3,2,1,0:T(4,128)(2,1)S(1)}, u32[]{:S(2)}, u32[]{:S(2)}) %all-to-all-start.2) | async-done | bytes 2211872 | tf_op jit(solution)/shard_map/all_to_all | solution.py:488
  344.9 4.1 %all-to-all-start.3 = ((bf16[32,8,2880]{2,1,0:T(8,128)(2,1)}), bf16[32,8,2880]{2,1,0:T(8,128)(2,1)}, u32[]{:S(2)}, u32[]{:S(2)}) async-start(bf16[32,8,2880]{2,1,0:T(8,128)(2,1)} %bitcast.29), calls=%async_computation.3 | async-start | bytes 3014656 | tf_op jit(solution)/shard_map/all_to_all | solution.py:488
  349.1 2.5 reshape.267
  351.5 2.6 fusion.55
  354.2 31.2 %all-to-all-done.3 = bf16[32,8,2880]{2,1,0:T(8,128)(2,1)} async-done(((bf16[32,8,2880]{2,1,0:T(8,128)(2,1)}), bf16[32,8,2880]{2,1,0:T(8,128)(2,1)}, u32[]{:S(2)}, u32[]{:S(2)}) %all-to-all-start.3) | async-done | bytes 1474592 | tf_op jit(solution)/shard_map/all_to_all | solution.py:488
  385.4 2.0 fusion
  (120 shorter events, 42.8 us)
Async XLA Ops:
  6.5 108.2 %all-gather.3.cloned.1.call-start = ((), (), s32[]{:S(2)}) async-start(), calls=%async_computation.4 | async-start | bytes 7077888 | tf_op jit(solution)/shard_map/all_gather | solution.py:352
  10.0 7.1 %copy-start.11 = (bf16[2880,128]{1,0:T(8,128)(2,1)S(1)}, bf16[2880,128]{1,0:T(8,128)(2,1)}, u32[]{:S(2)}) copy-start(bf16[2880,128]{1,0:T(8,128)(2,1)} %param.19) | copy-start | bytes 2211844
  10.9 10.7 %collective-permute-start = (bf16[96,1024]{1,0:T(8,128)(2,1)}, bf16[96,1024]{1,0:T(8,128)(2,1)}, u32[]{:S(2)}, u32[]{:S(2)}) collective-permute-start(bf16[96,1024]{1,0:T(8,128)(2,1)} %get-tuple-element.73), channel_id=1, source_target_pairs={{0,24},{1,25},{2,26},{3,27},{4,28},{5,29},{6,30},{7,31},{8,0},{9,1... | collective-permute-start | bytes 589832 | tf_op jit(solution)/shard_map/ppermute | solution.py:293
  15.9 17.0 %collective-permute-start.1 = (bf16[96,1024]{1,0:T(8,128)(2,1)}, bf16[96,1024]{1,0:T(8,128)(2,1)}, u32[]{:S(2)}, u32[]{:S(2)}) collective-permute-start(bf16[96,1024]{1,0:T(8,128)(2,1)} %get-tuple-element.72), channel_id=1, source_target_pairs={{0,16},{1,17},{2,18},{3,19},{4,20},{5,21},{6,22},{7,23},{8,24},{9,... | collective-permute-start | bytes 589832 | tf_op jit(solution)/shard_map/ppermute | solution.py:293
  15.9 18.0 %collective-permute-start.2 = (bf16[96,1024]{1,0:T(8,128)(2,1)}, bf16[96,1024]{1,0:T(8,128)(2,1)}, u32[]{:S(2)}, u32[]{:S(2)}) collective-permute-start(bf16[96,1024]{1,0:T(8,128)(2,1)} %get-tuple-element.71), channel_id=1, source_target_pairs={{0,8},{1,9},{2,10},{3,11},{4,12},{5,13},{6,14},{7,15},{8,16},{9,17... | collective-permute-start | bytes 589832 | tf_op jit(solution)/shard_map/ppermute | solution.py:293
  17.2 21.5 %collective-permute-start.3 = (bf16[3616,128]{1,0:T(8,128)(2,1)S(1)}, bf16[3616,128]{1,0:T(8,128)(2,1)S(1)}, u32[]{:S(2)}, u32[]{:S(2)}) collective-permute-start(bf16[3616,128]{1,0:T(8,128)(2,1)S(1)} %pad_maximum_fusion.refs_4_), channel_id=1, source_target_pairs={{0,2},{1,3},{2,0},{3,1},{4,6},{5,7},{6,4},{7,5},{8,10},{9,11},{10,... | collective-permute-start | bytes 2777096 | tf_op jit(solution)/shard_map/ppermute | solution.py:306
  36.8 7.3 %copy-start.3 = (s32[4]{0:T(128)S(1)}, s32[4]{0:T(128)}, u32[]{:S(2)}) copy-start(s32[4]{0:T(128)} %constant.183.clone) | copy-start | bytes 52
  37.7 7.7 %copy-start.17 = (s32[128,4]{0,1:T(4,128)S(1)}, s32[128,4]{0,1:T(4,128)}, u32[]{:S(2)}) copy-start(s32[128,4]{0,1:T(4,128)} %param.15) | copy-start | bytes 6148
  37.7 7.7 %copy-start.18 = (f32[128,4]{0,1:T(4,128)S(1)}, f32[128,4]{0,1:T(4,128)}, u32[]{:S(2)}) copy-start(f32[128,4]{0,1:T(4,128)} %param.16) | copy-start | bytes 6148
  38.8 37.5 %copy-start.19 = (f32[64]{0:T(128)S(1)}, f32[64]{0:T(128)}, u32[]{:S(2)}) copy-start(f32[64]{0:T(128)} %param.22) | copy-start | bytes 772
  38.8 50.0 %collective-permute-start.4 = (bf16[3616,128]{1,0:T(8,128)(2,1)S(1)}, bf16[3616,128]{1,0:T(8,128)(2,1)}, u32[]{:S(2)}, u32[]{:S(2)}) collective-permute-start(bf16[3616,128]{1,0:T(8,128)(2,1)S(1)} %pad_maximum_fusion.refs_4_), channel_id=1, source_target_pairs={{0,4},{1,5},{2,6},{3,7},{4,0},{5,1},{6,2},{7,3},{8,12},{9,13},{10,... | collective-permute-start | bytes 2777096 | tf_op jit(solution)/shard_map/ppermute | solution.py:306
  40.4 18.3 %collective-permute-start.5 = (bf16[2880,128]{1,0:T(8,128)(2,1)S(1)}, bf16[2880,128]{1,0:T(8,128)(2,1)}, u32[]{:S(2)}, u32[]{:S(2)}) collective-permute-start(bf16[2880,128]{1,0:T(8,128)(2,1)S(1)} %fusion.15.refs_0_), channel_id=1, source_target_pairs={{0,8},{1,9},{2,10},{3,11},{4,12},{5,13},{6,14},{7,15},{8,24},{9,25... | collective-permute-start | bytes 2211848 | tf_op jit(solution)/shard_map/ppermute | solution.py:299
  46.6 13.4 %copy-start.8 = (f32[256,384]{1,0:T(8,128)}, f32[256,384]{1,0:T(8,128)S(1)}, u32[]{:S(2)}) copy-start(f32[256,384]{1,0:T(8,128)S(1)} %fusion.24) | copy-start | bytes 1179652
  58.7 17.6 %collective-permute-start.6 = (bf16[2880,128]{1,0:T(8,128)(2,1)}, bf16[2880,128]{1,0:T(8,128)(2,1)}, u32[]{:S(2)}, u32[]{:S(2)}) collective-permute-start(bf16[2880,128]{1,0:T(8,128)(2,1)} %collective-permute-done.5.refs_1_), channel_id=1, source_target_pairs={{0,8},{1,9},{2,10},{3,11},{4,12},{5,13},{6,14},{7,15},{8,24},{9,25... | collective-permute-start | bytes 2211848 | tf_op jit(solution)/shard_map/ppermute | solution.py:299
  60.2 29.2 %collective-permute-start.7 = (bf16[3616,128]{1,0:T(8,128)(2,1)S(1)}, bf16[3616,128]{1,0:T(8,128)(2,1)}, u32[]{:S(2)}, u32[]{:S(2)}) collective-permute-start(bf16[3616,128]{1,0:T(8,128)(2,1)S(1)} %pad_maximum_fusion.refs_4_), channel_id=1, source_target_pairs={{0,6},{1,7},{2,4},{3,5},{4,2},{5,3},{6,0},{7,1},{8,14},{9,15},{10,... | collective-permute-start | bytes 2777096 | tf_op jit(solution)/shard_map/ppermute | solution.py:306
  76.2 16.7 %collective-permute-start.8 = (bf16[2880,128]{1,0:T(8,128)(2,1)}, bf16[2880,128]{1,0:T(8,128)(2,1)}, u32[]{:S(2)}, u32[]{:S(2)}) collective-permute-start(bf16[2880,128]{1,0:T(8,128)(2,1)} %collective-permute-done.6.refs_2_), channel_id=1, source_target_pairs={{0,8},{1,9},{2,10},{3,11},{4,12},{5,13},{6,14},{7,15},{8,24},{9,25... | collective-permute-start | bytes 2211848 | tf_op jit(solution)/shard_map/ppermute | solution.py:299
  80.3 12.6 %collective-permute-start.9 = (bf16[3616,128]{1,0:T(8,128)(2,1)S(1)}, bf16[3616,128]{1,0:T(8,128)(2,1)S(1)}, u32[]{:S(2)}, u32[]{:S(2)}) collective-permute-start(bf16[3616,128]{1,0:T(8,128)(2,1)S(1)} %pad_maximum_fusion.refs_4_), channel_id=1, source_target_pairs={{0,1},{1,0},{2,3},{3,2},{4,5},{5,4},{6,7},{7,6},{8,9},{9,8},{10,11... | collective-permute-start | bytes 2777096 | tf_op jit(solution)/shard_map/ppermute | solution.py:306
  88.8 4.1 %collective-permute-start.10 = (bf16[3616,128]{1,0:T(8,128)(2,1)S(1)}, bf16[3616,128]{1,0:T(8,128)(2,1)S(1)}, u32[]{:S(2)}, u32[]{:S(2)}) collective-permute-start(bf16[3616,128]{1,0:T(8,128)(2,1)S(1)} %collective-permute-done.3.refs_6_), channel_id=1, source_target_pairs={{0,1},{1,0},{2,3},{3,2},{4,5},{5,4},{6,7},{7,6},{8,9},{9,8},{10,11... | collective-permute-start | bytes 2777096 | tf_op jit(solution)/shard_map/ppermute | solution.py:306
  88.8 4.1 %collective-permute-start.11 = (bf16[3616,128]{1,0:T(8,128)(2,1)}, bf16[3616,128]{1,0:T(8,128)(2,1)S(1)}, u32[]{:S(2)}, u32[]{:S(2)}) collective-permute-start(bf16[3616,128]{1,0:T(8,128)(2,1)} %collective-permute-done.4.refs_8_), channel_id=1, source_target_pairs={{0,1},{1,0},{2,3},{3,2},{4,5},{5,4},{6,7},{7,6},{8,9},{9,8},{10,11... | collective-permute-start | bytes 2777096 | tf_op jit(solution)/shard_map/ppermute | solution.py:306
  92.9 3.5 collective-permute-start.12
  104.7 10.0 %copy-start.1 = (bf16[4,128,256]{2,1,0:T(8,128)(2,1)}, bf16[4,128,256]{2,1,0:T(8,128)(2,1)S(1)}, u32[]{:S(2)}) copy-start(bf16[4,128,256]{2,1,0:T(8,128)(2,1)S(1)} %get-tuple-element.51.key_values_ref) | copy-start | bytes 786436
  104.7 10.0 %collective-permute-start.13 = (bf16[4,128,256]{2,1,0:T(8,128)(2,1)S(1)}, bf16[4,128,256]{2,1,0:T(8,128)(2,1)S(1)}, u32[]{:S(2)}, u32[]{:S(2)}) collective-permute-start(bf16[4,128,256]{2,1,0:T(8,128)(2,1)S(1)} %get-tuple-element.51.key_values_ref), channel_id=1, source_target_pairs={{0,1},{1,2},{2,3},{3,4},{4,5},{5,6},{6,7},{7,0},{8,9},{9,10},{10,1... | collective-permute-start | bytes 786440 | tf_op jit(solution)/shard_map/ppermute | solution.py:303
  124.2 19.4 %collective-permute-start.14 = (bf16[2880,128]{1,0:T(8,128)(2,1)S(1)}, bf16[2880,128]{1,0:T(8,128)(2,1)S(1)}, u32[]{:S(2)}, u32[]{:S(2)}) collective-permute-start(bf16[2880,128]{1,0:T(8,128)(2,1)S(1)} %convert_bitcast_fusion), channel_id=1, source_target_pairs={{0,8},{1,9},{2,10},{3,11},{4,12},{5,13},{6,14},{7,15},{8,24},{9,25... | collective-permute-start | bytes 2211848 | tf_op jit(solution)/shard_map/ppermute | solution.py:299
  145.1 37.7 %copy-start.7 = (bf16[128,2880]{0,1:T(8,128)(2,1)S(1)}, bf16[128,2880]{0,1:T(8,128)(2,1)}, u32[]{:S(2)}) copy-start(bf16[128,2880]{0,1:T(8,128)(2,1)} %param.14) | copy-start | bytes 2211844
  145.1 18.5 %collective-permute-start.15 = (bf16[2880,128]{1,0:T(8,128)(2,1)S(1)}, bf16[2880,128]{1,0:T(8,128)(2,1)S(1)}, u32[]{:S(2)}, u32[]{:S(2)}) collective-permute-start(bf16[2880,128]{1,0:T(8,128)(2,1)S(1)} %fusion.12), channel_id=1, source_target_pairs={{0,8},{1,9},{2,10},{3,11},{4,12},{5,13},{6,14},{7,15},{8,24},{9,25... | collective-permute-start | bytes 2211848 | tf_op jit(solution)/shard_map/ppermute | solution.py:299
  165.2 20.3 %copy-start.16 = (f32[2880]{0:T(1024)S(1)}, f32[2880]{0:T(1024)}, u32[]{:S(2)}) copy-start(f32[2880]{0:T(1024)} %param.18) | copy-start | bytes 34564
  165.2 17.6 %collective-permute-start.16 = (bf16[2880,128]{1,0:T(8,128)(2,1)S(1)}, bf16[2880,128]{1,0:T(8,128)(2,1)S(1)}, u32[]{:S(2)}, u32[]{:S(2)}) collective-permute-start(bf16[2880,128]{1,0:T(8,128)(2,1)S(1)} %fusion.10), channel_id=1, source_target_pairs={{0,8},{1,9},{2,10},{3,11},{4,12},{5,13},{6,14},{7,15},{8,24},{9,25... | collective-permute-start | bytes 2211848 | tf_op jit(solution)/shard_map/ppermute | solution.py:299
  188.8 57.8 %all-to-all-start = ((bf16[32,3,4,2880]{3,2,1,0:T(4,128)(2,1)}), bf16[32,3,4,2880]{3,2,1,0:T(4,128)(2,1)S(1)}, u32[]{:S(2)}, u32[]{:S(2)}) async-start(bf16[32,3,4,2880]{3,2,1,0:T(4,128)(2,1)} %reshape.261), calls=%async_computation | async-start | bytes 4521984 | tf_op jit(solution)/shard_map/all_to_all | solution.py:488
  246.6 40.5 %all-to-all-start.1 = ((bf16[32,8,2880]{2,1,0:T(8,128)(2,1)}), bf16[32,8,2880]{2,1,0:T(8,128)(2,1)}, u32[]{:S(2)}, u32[]{:S(2)}) async-start(bf16[32,8,2880]{2,1,0:T(8,128)(2,1)} %bitcast.25), calls=%async_computation.1 | async-start | bytes 3014656 | tf_op jit(solution)/shard_map/all_to_all | solution.py:488
  287.1 57.8 %all-to-all-start.2 = ((bf16[32,3,4,2880]{3,2,1,0:T(4,128)(2,1)}), bf16[32,3,4,2880]{3,2,1,0:T(4,128)(2,1)S(1)}, u32[]{:S(2)}, u32[]{:S(2)}) async-start(bf16[32,3,4,2880]{3,2,1,0:T(4,128)(2,1)} %reshape.264), calls=%async_computation.2 | async-start | bytes 4521984 | tf_op jit(solution)/shard_map/all_to_all | solution.py:488
  344.9 40.5 %all-to-all-start.3 = ((bf16[32,8,2880]{2,1,0:T(8,128)(2,1)}), bf16[32,8,2880]{2,1,0:T(8,128)(2,1)}, u32[]{:S(2)}, u32[]{:S(2)}) async-start(bf16[32,8,2880]{2,1,0:T(8,128)(2,1)} %bitcast.29), calls=%async_computation.3 | async-start | bytes 3014656 | tf_op jit(solution)/shard_map/all_to_all | solution.py:488
  351.5 33.9 %copy-start.12 = (bf16[256,256]{1,0:T(8,128)(2,1)S(1)}, bf16[256,256]{1,0:T(8,128)(2,1)}, u32[]{:S(2)}) copy-start(bf16[256,256]{1,0:T(8,128)(2,1)} %fusion.21) | copy-start | bytes 393220
  (10 other events, 32.9 us)
Sparse Core Ops, SparseCore 0:
  38.9 75.2 all-gather.2
where the time goes:
time: 403 us; the launch traced here: 396 us
  waiting for transfers between devices  213 us (53%)
  Pallas kernels  85.1 us (21%)
  starting transfers between devices  37.4 us (9%)
  local copies, waits for them, and re-layouts  25.1 us (6%)
  other arithmetic  15.8 us (4%)
  between operations  14.3 us (4%)
  matrix products  5.34 us (1%)
    all_to_all x4, waiting for transfers between devices, exchange(): return lax.all_to_all(parts, 'ctx', split_axis=0, concat_axis=0, tiled=True)  112 us
    ppermute x6, waiting for transfers between devices, pass_on(): return lax.ppermute(block, 'ctx', route)  66 us
    pallas_call x2, Pallas kernels, run_expert(): pl.pallas_call(functools.partial(expert_kernel, tile, hidden), grid=(-(-h...  52.6 us
    pallas_call x2, Pallas kernels, attend_and_project(): pl.pallas_call(functools.partial(attend_kernel, numbers), in_specs=[smem,...  22.8 us
    all_to_all x4, starting transfers between devices, exchange(): return lax.all_to_all(parts, 'ctx', split_axis=0, concat_axis=0, tiled=True)  19 us
    ppermute x3, waiting for transfers between devices, shift(): lax.ppermute(block, 'ctx', [(i, (i + steps * PLANE) % n_ctx) for i in ran...  13.2 us
    ppermute x7, waiting for transfers between devices, swap(): return lax.ppermute(block, 'ctx', [(i, i ^ bits) for i in range(n_ctx)])  12 us
    ppermute x1, waiting for transfers between devices, behind(): return lax.ppermute(block, 'ctx', route)  9.75 us
  transfers between devices with their start and end apart: 22, of which 15 were waited for; matrix products, arithmetic and copies ran while one was open for 7% of the time, Pallas kernels for 19%

commit v1 on v0

--- a/solution.py
+++ b/solution.py
@@ -120,71 +120,101 @@
     return values * cosine + partner * signed_sine
 
 
-def qkv_kernel(count, place_ref, *refs):
-    blocks, shares, refs = refs[:count], refs[count : count + PLANE], refs[count + PLANE :]
-    cos_ref, sin_ref, q_ref, key_value_ref, rows_ref, kv_ref = refs
+def kv_kernel(count, *refs):
+    blocks, (weights_hbm, cos_ref, sin_ref, rows_ref, key_value_ref, weight_ref, kv_ref, copied) = refs[:count], refs[count:]
     width, rows = blocks[0].shape
-    cols = shares[0].shape[1]
-    share = kv_ref.shape[2]
+    planes, packed_rows, cols = weight_ref.shape
+    copy = pltpu.make_async_copy(weights_hbm.at[:, width : width + packed_rows], weight_ref, copied)
+    copy.start()
     for r in range(count):
         rows_ref[r * rows : (r + 1) * rows, :] = blocks[r][...].T
-
-    for i in range(PLANE):
-        for tile in range(-(-width // cols)):
-            at, lanes = width + 2 * share * tile, slice(tile * cols, (tile + 1) * cols)
+    copy.wait()
+    share = kv_ref.shape[2]
+    for p in range(planes):
+        for tile in range(packed_rows // (2 * share)):
+            at, lanes = 2 * share * tile, slice(tile * cols, (tile + 1) * cols)
             for part in range(2):
-                kv_ref[part, place_ref[i], :, lanes] = shares[i][at + part * share : at + (part + 1) * share]
-    both = kv_ref[...].reshape(2 * PLANE * share, kv_ref.shape[3])[:, :width]
+                kv_ref[part, p, :, lanes] = weight_ref[p, at + part * share : at + (part + 1) * share]
+    both = kv_ref[...].reshape(2 * planes * share, kv_ref.shape[3])[:, :width]
     lines = dot_nt(rows_ref[...], both)
-    half = PLANE * share
+    half = planes * share
     for r in range(count):
         piece = lines[r * rows : (r + 1) * rows]
         key_value_ref[r, :, :half] = turn(piece[:, :half], cos_ref[r], sin_ref[r]).astype(BF16)
         key_value_ref[r, :, half:] = piece[:, half:].astype(BF16)
 
-    for i in range(0, PLANE, 2):
-        weight = jnp.concatenate([shares[i][:width], shares[i + 1][:width]], axis=1)
-        query = dot32(rows_ref[...], weight)
+
+def project_keys(blocks, weights, share, cosine, signed_sine):
+    count = len(blocks)
+    width, rows = blocks[0].shape
+    planes, packed, cols = weights.shape
+    kv_cols = 2 * planes * share
+    vmem = pl.BlockSpec(memory_space=pltpu.VMEM)
+    return pl.pallas_call(
+        functools.partial(kv_kernel, count),
+        in_specs=[vmem] * count + [pl.BlockSpec(memory_space=pl.ANY), vmem, vmem],
+        out_specs=[vmem, vmem],
+        out_shape=[
+            jax.ShapeDtypeStruct((count * rows, width), BF16),
+            jax.ShapeDtypeStruct((count, rows, kv_cols), BF16),
+        ],
+        scratch_shapes=[
+            pltpu.VMEM((planes, packed - width, cols), BF16),
+            pltpu.VMEM((2, planes, share, (packed - width) // (2 * share) * cols), BF16),
+            pltpu.SemaphoreType.DMA,
+        ],
+        compiler_params=pltpu.CompilerParams(vmem_limit_bytes=40 * 2**20),
+        cost_estimate=pl.CostEstimate(
+            flops=2 * count * rows * width * kv_cols,
+            bytes_accessed=2 * width * (kv_cols + 2 * count * rows),
+            transcendentals=0,
+        ),
+    )(*blocks, weights, cosine, signed_sine)
+
+
+def query_kernel(rows_ref, weights_hbm, cos_ref, sin_ref, q_ref, weight_ref, copied):
+    count, rows = q_ref.shape[:2]
+    planes, width, cols = weight_ref.shape
+    copies = [
+        pltpu.make_async_copy(weights_hbm.at[p : p + 2, :width], weight_ref.at[p : p + 2], copied.at[p // 2])
+        for p in range(0, planes, 2)
+    ]
+    for copy in copies:
+        copy.start()
+    for p in range(0, planes, 2):
+        copies[p // 2].wait()
+        query = dot32(rows_ref[...], jnp.concatenate([weight_ref[p], weight_ref[p + 1]], axis=1))
         for k in range(2):
-            lanes = pl.ds(pl.multiple_of(place_ref[i + k] * cols, cols), cols)
+            lanes = slice((p + k) * cols, (p + k + 1) * cols)
             for r in range(count):
                 piece = query[r * rows : (r + 1) * rows, k * cols : (k + 1) * cols]
                 q_ref[r, :, lanes] = turn(piece, cos_ref[r], sin_ref[r]).astype(BF16)
 
 
-def project_blocks(place, blocks, shares, share, cosine, signed_sine):
-    count = len(blocks)
-    width, rows = blocks[0].shape
-    cols = shares[0].shape[1]
-    tiles = -(-width // cols)
-    kv_cols = 2 * PLANE * share
+def project_queries(lines, weights, cosine, signed_sine):
+    count, rows, _ = cosine.shape
+    width = lines.shape[1]
+    planes, _, cols = weights.shape
     vmem = pl.BlockSpec(memory_space=pltpu.VMEM)
     return pl.pallas_call(
-        functools.partial(qkv_kernel, count),
-        in_specs=[pl.BlockSpec(memory_space=pltpu.SMEM)] + [vmem] * (count + PLANE + 2),
-        out_specs=[vmem, vmem],
-        out_shape=[
-            jax.ShapeDtypeStruct((count, rows, PLANE * cols), BF16),
-            jax.ShapeDtypeStruct((count, rows, kv_cols), BF16),
-        ],
-        scratch_shapes=[
-            pltpu.VMEM((count * rows, width), BF16),
-            pltpu.VMEM((2, PLANE, share, tiles * cols), BF16),
-        ],
+        query_kernel,
+        in_specs=[vmem, pl.BlockSpec(memory_space=pl.ANY), vmem, vmem],
+        out_specs=vmem,
+        out_shape=jax.ShapeDtypeStruct((count, rows, planes * cols), BF16),
+        scratch_shapes=[pltpu.VMEM((planes, width, cols), BF16), pltpu.SemaphoreType.DMA((planes // 2,))],
         compiler_params=pltpu.CompilerParams(vmem_limit_bytes=40 * 2**20),
         cost_estimate=pl.CostEstimate(
-            flops=2 * count * rows * width * (PLANE * cols + kv_cols),
-            bytes_accessed=2 * width * (PLANE * cols + kv_cols + count * rows),
+            flops=2 * count * rows * width * planes * cols,
+            bytes_accessed=2 * width * (planes * cols + count * rows),
             transcendentals=0,
         ),
-    )(place, *blocks, *shares, cosine, signed_sine)
+    )(lines, weights, cosine, signed_sine)
 
 
 def attend_kernel(
-    numbers, place_ref, sinks_ref, queries_ref, key_values_ref, halos_ref, weight_hbm, out_ref, att_ref, weight_ref, copied
+    numbers, pieces, place_ref, sinks_ref, queries_ref, key_values_ref, halos_ref, *refs
 ):
-    copy = pltpu.make_async_copy(weight_hbm, weight_ref, copied)
-    copy.start()
+    share_refs, (out_ref, att_ref, total_ref) = refs[: len(pieces)], refs[len(pieces) :]
     count, rows = key_values_ref.shape[:2]
     pair = 2 * HD
     kv_heads = key_values_ref.shape[2] // pair
@@ -239,41 +269,44 @@
             mixed = mixed + dot32(jnp.concatenate(probs_previous, axis=1), previous[head][1])
             att_ref[i * rows : (i + 1) * rows, p * pair : (p + 1) * pair] = mixed.astype(BF16)
 
-    shares, groups, padded, depth = weight_ref.shape
+    groups, shares, padded, _ = total_ref.shape
     cols = out_ref.shape[1] // (shares * groups)
     attended = att_ref[...]
-    copy.wait()
-    for p in range(shares):
-        terms = dot_nt(weight_ref[p].reshape(groups * padded, depth), attended)
-        for g in range(groups):
+    for (relative, first), weight_ref in zip(pieces, share_refs):
+        size, _, depth = weight_ref.shape
+        terms = dot_nt(weight_ref[...].reshape(size * padded, depth), attended)
+        for g in range(size):
+            total_ref[first + g, place_ref[2 * count + relative]] = terms[g * padded : (g + 1) * padded]
+    for g in range(groups):
+        for p in range(shares):
             at = (g * shares + p) * cols
             for i in range(len(numbers)):
-                out_ref[i, at : at + cols, :] = terms[g * padded : g * padded + cols, i * rows : (i + 1) * rows]
-
-
-def attend_and_project(numbers, place, sinks, queries, key_values, halos, weight, width):
+                out_ref[i, at : at + cols, :] = total_ref[g, p, :cols, i * rows : (i + 1) * rows]
+
+
+def attend_and_project(numbers, place, sinks, queries, key_values, halos, shares, width):
     rows = queries.shape[1]
     count = len(numbers)
-    depth = weight.shape[3]
+    groups, padded, depth = shares[0][2].shape
+    pieces = tuple((relative, first) for relative, first, _ in shares)
     vmem = pl.BlockSpec(memory_space=pltpu.VMEM)
     smem = pl.BlockSpec(memory_space=pltpu.SMEM)
     return pl.pallas_call(
-        functools.partial(attend_kernel, numbers),
-        in_specs=[smem, smem] + [vmem] * 3 + [pl.BlockSpec(memory_space=pl.ANY)],
+        functools.partial(attend_kernel, numbers, pieces),
+        in_specs=[smem, smem] + [vmem] * (3 + len(shares)),
         out_specs=vmem,
         out_shape=jax.ShapeDtypeStruct((count, width, rows), F32),
         scratch_shapes=[
             pltpu.VMEM((count * rows, depth), BF16),
-            pltpu.VMEM(weight.shape, BF16),
-            pltpu.SemaphoreType.DMA,
+            pltpu.VMEM((groups, PLANE, padded, count * rows), F32),
         ],
-        compiler_params=pltpu.CompilerParams(vmem_limit_bytes=56 * 2**20),
+        compiler_params=pltpu.CompilerParams(vmem_limit_bytes=40 * 2**20),
         cost_estimate=pl.CostEstimate(
             flops=2 * count * rows * depth * (width + 8 * rows),
             bytes_accessed=2 * width * (depth + 2 * count * rows),
             transcendentals=count * rows * rows * depth // HD,
         ),
-    )(place, sinks, queries, key_values, halos, weight)
+    )(place, sinks, queries, key_values, halos, *[weight for _, _, weight in shares])
 
 
 def project_planes(
@@ -316,7 +349,7 @@
     packed = jnp.concatenate(
         [query_weight, kv_rows.transpose(1, 0, 2).reshape(tiles * 2 * share, lanes)], axis=0
     )
-    near, far = swap(packed, 2), swap(packed, 4)
+    weights = lax.all_gather(packed, "ctx", axis_index_groups=planes)
 
     cols = out_weight.shape[1]
     padded = -(-cols // 16) * 16
@@ -347,25 +380,27 @@
     below = (places[jnp.maximum(block_z - 1, 0)] - mine) % n_z
     previous_at = jnp.where(j == 0, below, jnp.arange(n_z, dtype=jnp.int32))
     relative = jnp.arange(PLANE, dtype=jnp.int32) ^ j
-    place = jnp.concatenate([(numbers == 0).astype(jnp.int32), previous_at])
-    out_mine, near = lax.optimization_barrier((out_mine, near))
-    out_all = lax.all_gather(out_mine, "ctx", axis_index_groups=planes)
+    place = jnp.concatenate([(numbers == 0).astype(jnp.int32), previous_at, relative])
     for _ in range(n_z - 2):
         blocks.append(pass_on(blocks[-1]))
-    packed, blocks[1] = lax.optimization_barrier((packed, blocks[1]))
-    corner = swap(packed, 6)
-    second = min(2, n_z - 1)
-    (near, far, blocks[second], cosine, signed_sine, place, relative, sinks, early) = lax.optimization_barrier(
-        (near, far, blocks[second], cosine, signed_sine, place, relative, sinks, early)
-    )
-    shares = [packed, swap(packed, 1), near, swap(near, 1), far, swap(far, 1)]
-    corner, blocks[-1] = lax.optimization_barrier((corner, blocks[-1]))
-    shares += [corner, swap(corner, 1)]
-    queries, key_values = project_blocks(relative, blocks, shares, share, cosine, signed_sine)
+    (blocks[1], cosine, signed_sine, place, sinks, early) = lax.optimization_barrier(
+        (blocks[1], cosine, signed_sine, place, sinks, early)
+    )
+    cut = n_z // 2
+    near, far = swap(out_mine, 2), swap(out_mine, 4)
+    corner_low, corner_high = swap(near[:cut], 4), swap(far[cut:], 2)
+    (near, far, corner_low, corner_high, blocks[-1]) = lax.optimization_barrier(
+        (near, far, corner_low, corner_high, blocks[-1])
+    )
+    shares = []
+    for r, first, piece in ((0, 0, out_mine), (2, 0, near), (4, 0, far), (6, 0, corner_low), (6, cut, corner_high)):
+        shares += [(r, first, piece), (r + 1, first, swap(piece, 1))]
+    lines, key_values = project_keys(blocks, weights, share, cosine, signed_sine)
     halos = behind(key_values)
+    queries = project_queries(lines, weights, cosine, signed_sine)
 
     def parts_of(numbers):
-        return attend_and_project(numbers, place, sinks, queries, key_values, halos, out_all, width)
+        return attend_and_project(numbers, place, sinks, queries, key_values, halos, shares, width)
 
     running = parts_of((1,))[0].astype(BF16)
     others = parts_of(tuple(range(2, n_z)) + (0,))

time: 403 us -> 403 us (level)
  waiting for transfers between devices: 213 us -> 201 us
  local copies, waits for them, and re-layouts: 25.1 us -> 32.8 us
    ppermute x1, waiting for transfers between devices: 9.75 us -> 0.01 us  [behind(): return lax.ppermute(block, 'ctx', route)]
    unnamed x46 -> x70, local copies, waits for them, and re-layouts: 7.34 us -> 16 us
    ppermute x3, waiting for transfers between devices: 13.2 us -> 8.28 us  [shift(): lax.ppermute(block, 'ctx', [(i, (i + steps * PLANE) % n_ctx) for i in ran...]
    pallas_call x3 -> x4, Pallas kernels: 30.1 us -> 32.8 us  [the longest x2 20.7 us: attend_and_project(): pl.pallas_call(functools.partial(attend_kernel, numbers, pieces), in_spec...]
    ppermute x7 -> x9, waiting for transfers between devices: 12 us -> 13.7 us  [swap(): return lax.ppermute(block, 'ctx', [(i, i ^ bits) for i in range(n_ctx)])]
  transfers between devices with their start and end apart: 22 -> 24, of which waited for: 15 -> 12; matrix products, arithmetic and copies ran while one was open for 7% -> 8% of each run, Pallas kernels for 19% -> 20%
where the time goes in v1:
time: 403 us; the launch traced here: 397 us
  waiting for transfers between devices  201 us (50%)
  Pallas kernels  87.9 us (22%)
  starting transfers between devices  39.4 us (10%)
  local copies, waits for them, and re-layouts  32.8 us (8%)
  other arithmetic  15.6 us (4%)
  between operations  14.3 us (4%)
  matrix products  6.16 us (2%)
    all_to_all x4, waiting for transfers between devices, exchange(): return lax.all_to_all(parts, 'ctx', split_axis=0, concat_axis=0, tiled=True)  111 us
    ppermute x6, waiting for transfers between devices, pass_on(): return lax.ppermute(block, 'ctx', route)  67.9 us
    pallas_call x2, Pallas kernels, run_expert(): pl.pallas_call(functools.partial(expert_kernel, tile, hidden), grid=(-(-h...  52.6 us
    pallas_call x2, Pallas kernels, attend_and_project(): pl.pallas_call(functools.partial(attend_kernel, numbers, pieces), in_spec...  20.7 us
    all_to_all x4, starting transfers between devices, exchange(): return lax.all_to_all(parts, 'ctx', split_axis=0, concat_axis=0, tiled=True)  19.4 us
    unnamed x70, local copies, waits for them, and re-layouts  16 us
    ppermute x9, waiting for transfers between devices, swap(): return lax.ppermute(block, 'ctx', [(i, i ^ bits) for i in range(n_ctx)])  13.7 us
    pallas_call x1, Pallas kernels, project_queries(): pl.pallas_call(query_kernel, in_specs=[vmem, pl.BlockSpec(memory_space=pl...  8.72 us
  transfers between devices with their start and end apart: 24, of which 12 were waited for; matrix products, arithmetic and copies ran while one was open for 8% of the time, Pallas kernels for 20%

profile of v1, /device:TPU:0, one launch (start us, length us, event | category | flops | bytes accessed | tf_op | source)
XLA Modules:
  0.0 397.0 jit_solution(1473445592853484513)
XLA Ops:
  11.9 5.0 %collective-permute-start.2 = (bf16[96,1024]{1,0:T(8,128)(2,1)}, bf16[96,1024]{1,0:T(8,128)(2,1)S(1)}, u32[]{:S(2)}, u32[]{:S(2)}) collective-permute-start(bf16[96,1024]{1,0:T(8,128)(2,1)} %get-tuple-element.65), channel_id=1, source_target_pairs={{0,24},{1,25},{2,26},{3,27},{4,28},{5,29},{6,30},{7,31},{8,0},{9,1... | collective-permute-start | bytes 589832 | tf_op jit(solution)/shard_map/ppermute | solution.py:326
  18.0 2.5 collective-permute-start
  26.5 8.3 %collective-permute-done.3 = bf16[96,1024]{1,0:T(8,128)(2,1)S(1)} collective-permute-done((bf16[96,1024]{1,0:T(8,128)(2,1)}, bf16[96,1024]{1,0:T(8,128)(2,1)S(1)}, u32[]{:S(2)}, u32[]{:S(2)}) %collective-permute-start.3) | collective-permute-done | bytes 196640 | tf_op jit(solution)/shard_map/ppermute | solution.py:326
  34.9 14.7 %collective-permute-done.refs_1_ = bf16[2880,128]{1,0:T(8,128)(2,1)S(1)} collective-permute-done((bf16[2880,128]{1,0:T(8,128)(2,1)S(1)}, bf16[2880,128]{1,0:T(8,128)(2,1)S(1)}, u32[]{:S(2)}, u32[]{:S(2)}) %collective-permute-start) | collective-permute-done | bytes 737312 | tf_op jit(solution)/shard_map/ppermute | solution.py:332
  55.5 12.8 %collective-permute-done.1.refs_2_ = bf16[2880,128]{1,0:T(8,128)(2,1)} collective-permute-done((bf16[2880,128]{1,0:T(8,128)(2,1)S(1)}, bf16[2880,128]{1,0:T(8,128)(2,1)}, u32[]{:S(2)}, u32[]{:S(2)}) %collective-permute-start.1) | collective-permute-done | bytes 737312 | tf_op jit(solution)/shard_map/ppermute | solution.py:332
  71.4 5.8 %collective-permute-done.5.refs_2_ = bf16[4,96,1024]{2,1,0:T(8,128)(2,1)S(1)} collective-permute-done((bf16[4,96,1024]{2,1,0:T(8,128)(2,1)S(1)}, bf16[4,96,1024]{2,1,0:T(8,128)(2,1)S(1)}, u32[]{:S(2)}, u32[]{:S(2)}) %collective-permute-start.5) | collective-permute-done | bytes 786464 | tf_op jit(solution)/shard_map/ppermute | solution.py:339
  79.4 1.8 negate_select_fusion
  81.2 6.6 %collective-permute-done.7.refs_6_ = bf16[2,96,1024]{2,1,0:T(8,128)(2,1)} collective-permute-done((bf16[2,96,1024]{2,1,0:T(8,128)(2,1)S(1)}, bf16[2,96,1024]{2,1,0:T(8,128)(2,1)}, u32[]{:S(2)}, u32[]{:S(2)}) %collective-permute-start.7) | collective-permute-done | bytes 393248 | tf_op jit(solution)/shard_map/ppermute | solution.py:339
  93.6 3.1 copy-done
  101.0 3.4 shard_map.136
  106.7 1.8 copy-done.3
  109.4 8.7 %shard_map.137.queries_ref = bf16[4,128,1024]{2,1,0:T(8,128)(2,1)S(1)} custom-call(bf16[512,2880]{1,0:T(8,128)(2,1)S(1)} %copy-done.3, bf16[8,3616,128]{2,1,0:T(8,128)(2,1)S(1)} %bitcast.90, f32[4,128,128]{2,1,0:T(8,128)S(1)} %copy-done.7, f32[4,128,128]{2,1,0:T(8,128)S(1)} %get-tuple-element.38.refs_6_.sin_ref), custom_call_target="tpu_custom_call" | custom-call | flops 3019898880 | bytes 8847360 | tf_op jit(solution)/shard_map/pallas_call | solution.py:199
  118.2 6.6 %shard_map.138 = f32[1,2880,128]{2,1,0:T(8,128)S(1)} custom-call(s32[16]{0:T(128)S(1)} %pad_add_fusion.place_ref, f32[16]{0:T(128)S(1)} %dynamic_slice.24.sinks_ref, bf16[4,128,1024]{2,1,0:T(8,128)(2,1)S(1)} %shard_map.137.queries_ref, bf16[4,128,256]{2,1,0:T(8,128)(2,1)S(1)} %get-tuple-element.40.key_values_ref, ...), custom_call_target="tpu_custom_call" | custom-call | flops 1023410176 | bytes 7372800 | tf_op jit(solution)/shard_map/pallas_call | solution.py:294
  126.6 14.1 %shard_map.139 = f32[3,2880,128]{2,1,0:T(8,128)S(1)} custom-call(s32[16]{0:T(128)S(1)} %pad_add_fusion.place_ref, f32[16]{0:T(128)S(1)} %dynamic_slice.24.sinks_ref, bf16[4,128,1024]{2,1,0:T(8,128)(2,1)S(1)} %shard_map.137.queries_ref, bf16[4,128,256]{2,1,0:T(8,128)(2,1)S(1)} %get-tuple-element.40.key_values_ref, ...), custom_call_target="tpu_custom_call" | custom-call | flops 3070230528 | bytes 10321920 | tf_op jit(solution)/shard_map/pallas_call | solution.py:294
  140.7 4.3 %collective-permute-done.16 = bf16[2880,128]{1,0:T(8,128)(2,1)S(1)} collective-permute-done((bf16[2880,128]{1,0:T(8,128)(2,1)S(1)}, bf16[2880,128]{1,0:T(8,128)(2,1)S(1)}, u32[]{:S(2)}, u32[]{:S(2)}) %collective-permute-start.16) | collective-permute-done | bytes 737312 | tf_op jit(solution)/shard_map/ppermute | solution.py:332
  145.9 18.5 %collective-permute-done.17 = bf16[2880,128]{1,0:T(8,128)(2,1)S(1)} collective-permute-done((bf16[2880,128]{1,0:T(8,128)(2,1)S(1)}, bf16[2880,128]{1,0:T(8,128)(2,1)S(1)}, u32[]{:S(2)}, u32[]{:S(2)}) %collective-permute-start.17) | collective-permute-done | bytes 737312 | tf_op jit(solution)/shard_map/ppermute | solution.py:332
  165.2 17.6 %collective-permute-done.18 = bf16[2880,128]{1,0:T(8,128)(2,1)S(1)} collective-permute-done((bf16[2880,128]{1,0:T(8,128)(2,1)S(1)}, bf16[2880,128]{1,0:T(8,128)(2,1)S(1)}, u32[]{:S(2)}, u32[]{:S(2)}) %collective-permute-start.18) | collective-permute-done | bytes 737312 | tf_op jit(solution)/shard_map/ppermute | solution.py:332
  185.3 2.1 reshape.261
  187.4 4.9 %all-to-all-start = ((bf16[32,3,4,2880]{3,2,1,0:T(4,128)(2,1)}), bf16[32,3,4,2880]{3,2,1,0:T(4,128)(2,1)}, u32[]{:S(2)}, u32[]{:S(2)}) async-start(bf16[32,3,4,2880]{3,2,1,0:T(4,128)(2,1)} %reshape.261), calls=%async_computation | async-start | bytes 4521984 | tf_op jit(solution)/shard_map/all_to_all | solution.py:523
  194.0 50.6 %all-to-all-done = bf16[32,3,4,2880]{3,2,1,0:T(4,128)(2,1)} async-done(((bf16[32,3,4,2880]{3,2,1,0:T(4,128)(2,1)}), bf16[32,3,4,2880]{3,2,1,0:T(4,128)(2,1)}, u32[]{:S(2)}, u32[]{:S(2)}) %all-to-all-start) | async-done | bytes 2211872 | tf_op jit(solution)/shard_map/all_to_all | solution.py:523
  244.7 4.2 %all-to-all-start.1 = ((bf16[32,8,2880]{2,1,0:T(8,128)(2,1)}), bf16[32,8,2880]{2,1,0:T(8,128)(2,1)S(1)}, u32[]{:S(2)}, u32[]{:S(2)}) async-start(bf16[32,8,2880]{2,1,0:T(8,128)(2,1)} %bitcast.25), calls=%async_computation.1 | async-start | bytes 3014656 | tf_op jit(solution)/shard_map/all_to_all | solution.py:523
  248.9 4.3 %reshape.263.rows_ref = bf16[384,2880]{1,0:T(8,128)(2,1)} reshape(bf16[32,3,4,2880]{3,2,1,0:T(4,128)(2,1)} %all-to-all-done) | data formatting | bytes 4423680 | tf_op jit(solution)/shard_map/reshape | solution.py:544
  253.2 29.2 %shard_map.142 = bf16[384,2880]{1,0:T(8,128)(2,1)} custom-call(bf16[384,2880]{1,0:T(8,128)(2,1)} %reshape.263.rows_ref, bf16[2,2880,2880]{2,1,0:T(8,128)(2,1)} %bitcast.91, bf16[2,2880,2880]{2,1,0:T(8,128)(2,1)} %bitcast.92, bf16[2880,2880]{1,0:T(8,128)(2,1)} %bitcast.95), custom_call_target="tpu_custom_call" | custom-call | flops 19110297600 | bytes 54190080 | tf_op jit(solution)/shard_map/pallas_call | solution.py:445
  282.4 4.1 %reshape.264 = bf16[32,3,4,2880]{3,2,1,0:T(4,128)(2,1)} reshape(bf16[384,2880]{1,0:T(8,128)(2,1)} %shard_map.142) | data formatting | bytes 4423680 | tf_op jit(solution)/shard_map/reshape | solution.py:520
  287.6 6.2 %all-to-all-start.2 = ((bf16[32,3,4,2880]{3,2,1,0:T(4,128)(2,1)}), bf16[32,3,4,2880]{3,2,1,0:T(4,128)(2,1)S(1)}, u32[]{:S(2)}, u32[]{:S(2)}) async-start(bf16[32,3,4,2880]{3,2,1,0:T(4,128)(2,1)} %reshape.264), calls=%async_computation.2 | async-start | bytes 4521984 | tf_op jit(solution)/shard_map/all_to_all | solution.py:523
  293.8 23.4 %shard_map.143 = bf16[256,2880]{1,0:T(8,128)(2,1)} custom-call(bf16[256,2880]{1,0:T(8,128)(2,1)} %bitcast.97, bf16[2,2880,2880]{2,1,0:T(8,128)(2,1)} %bitcast.93, bf16[2,2880,2880]{2,1,0:T(8,128)(2,1)} %bitcast.94, bf16[2880,2880]{1,0:T(8,128)(2,1)} %bitcast.96), custom_call_target="tpu_custom_call" | custom-call | flops 12740198400 | bytes 52715520 | tf_op jit(solution)/shard_map/pallas_call | solution.py:445
  317.2 29.0 %all-to-all-done.2 = bf16[32,3,4,2880]{3,2,1,0:T(4,128)(2,1)S(1)} async-done(((bf16[32,3,4,2880]{3,2,1,0:T(4,128)(2,1)}), bf16[32,3,4,2880]{3,2,1,0:T(4,128)(2,1)S(1)}, u32[]{:S(2)}, u32[]{:S(2)}) %all-to-all-start.2) | async-done | bytes 2211872 | tf_op jit(solution)/shard_map/all_to_all | solution.py:523
  346.2 4.1 %all-to-all-start.3 = ((bf16[32,8,2880]{2,1,0:T(8,128)(2,1)}), bf16[32,8,2880]{2,1,0:T(8,128)(2,1)}, u32[]{:S(2)}, u32[]{:S(2)}) async-start(bf16[32,8,2880]{2,1,0:T(8,128)(2,1)} %bitcast.29), calls=%async_computation.3 | async-start | bytes 3014656 | tf_op jit(solution)/shard_map/all_to_all | solution.py:523
  350.3 2.5 reshape.267
  352.8 2.6 fusion.55
  355.5 31.2 %all-to-all-done.3 = bf16[32,8,2880]{2,1,0:T(8,128)(2,1)} async-done(((bf16[32,8,2880]{2,1,0:T(8,128)(2,1)}), bf16[32,8,2880]{2,1,0:T(8,128)(2,1)}, u32[]{:S(2)}, u32[]{:S(2)}) %all-to-all-start.3) | async-done | bytes 1474592 | tf_op jit(solution)/shard_map/all_to_all | solution.py:523
  386.7 2.0 fusion
  (152 shorter events, 46.6 us)
Async XLA Ops:
  6.5 87.1 %all-gather.3.cloned.1.call-start = ((), (), s32[]{:S(2)}) async-start(), calls=%async_computation.4 | async-start | bytes 8331264 | tf_op jit(solution)/shard_map/all_gather | solution.py:352
  11.0 12.0 %copy-start.30 = (f32[128,4]{0,1:T(4,128)S(1)}, f32[128,4]{0,1:T(4,128)}, u32[]{:S(2)}) copy-start(f32[128,4]{0,1:T(4,128)} %param.16) | copy-start | bytes 6148
  11.9 14.6 %collective-permute-start.2 = (bf16[96,1024]{1,0:T(8,128)(2,1)}, bf16[96,1024]{1,0:T(8,128)(2,1)S(1)}, u32[]{:S(2)}, u32[]{:S(2)}) collective-permute-start(bf16[96,1024]{1,0:T(8,128)(2,1)} %get-tuple-element.65), channel_id=1, source_target_pairs={{0,24},{1,25},{2,26},{3,27},{4,28},{5,29},{6,30},{7,31},{8,0},{9,1... | collective-permute-start | bytes 589832 | tf_op jit(solution)/shard_map/ppermute | solution.py:326
  17.0 17.8 %collective-permute-start.3 = (bf16[96,1024]{1,0:T(8,128)(2,1)}, bf16[96,1024]{1,0:T(8,128)(2,1)S(1)}, u32[]{:S(2)}, u32[]{:S(2)}) collective-permute-start(bf16[96,1024]{1,0:T(8,128)(2,1)} %get-tuple-element.64), channel_id=1, source_target_pairs={{0,16},{1,17},{2,18},{3,19},{4,20},{5,21},{6,22},{7,23},{8,24},{9,... | collective-permute-start | bytes 589832 | tf_op jit(solution)/shard_map/ppermute | solution.py:326
  17.0 17.9 %collective-permute-start.4 = (bf16[96,1024]{1,0:T(8,128)(2,1)S(1)}, bf16[96,1024]{1,0:T(8,128)(2,1)S(1)}, u32[]{:S(2)}, u32[]{:S(2)}) collective-permute-start(bf16[96,1024]{1,0:T(8,128)(2,1)S(1)} %get-tuple-element.63), channel_id=1, source_target_pairs={{0,8},{1,9},{2,10},{3,11},{4,12},{5,13},{6,14},{7,15},{8,16},{9,17... | collective-permute-start | bytes 589832 | tf_op jit(solution)/shard_map/ppermute | solution.py:326
  18.0 31.7 %collective-permute-start = (bf16[2880,128]{1,0:T(8,128)(2,1)S(1)}, bf16[2880,128]{1,0:T(8,128)(2,1)S(1)}, u32[]{:S(2)}, u32[]{:S(2)}) collective-permute-start(bf16[2880,128]{1,0:T(8,128)(2,1)S(1)} %fusion.15.refs_0_), channel_id=1, source_target_pairs={{0,8},{1,9},{2,10},{3,11},{4,12},{5,13},{6,14},{7,15},{8,24},{9,25... | collective-permute-start | bytes 2211848 | tf_op jit(solution)/shard_map/ppermute | solution.py:332
  24.1 26.4 %copy-start.20 = (f32[256,384]{1,0:T(8,128)}, f32[256,384]{1,0:T(8,128)S(1)}, u32[]{:S(2)}) copy-start(f32[256,384]{1,0:T(8,128)S(1)} %fusion.24) | copy-start | bytes 1179652
  34.9 19.5 %copy-start.28 = (f32[384]{0:T(512)S(1)}, f32[384]{0:T(512)}, u32[]{:S(2)}) copy-start(f32[384]{0:T(512)} %get-tuple-element.75) | copy-start | bytes 4612
  49.7 18.6 %collective-permute-start.1 = (bf16[2880,128]{1,0:T(8,128)(2,1)S(1)}, bf16[2880,128]{1,0:T(8,128)(2,1)}, u32[]{:S(2)}, u32[]{:S(2)}) collective-permute-start(bf16[2880,128]{1,0:T(8,128)(2,1)S(1)} %collective-permute-done.refs_1_), channel_id=1, source_target_pairs={{0,8},{1,9},{2,10},{3,11},{4,12},{5,13},{6,14},{7,15},{8,24},{9,25... | collective-permute-start | bytes 2211848 | tf_op jit(solution)/shard_map/ppermute | solution.py:332
  50.7 28.7 %copy-start.27 = (f32[4,128]{1,0:T(4,128)S(1)}, f32[4,128]{1,0:T(4,128)}, u32[]{:S(2)}) copy-start(f32[4,128]{1,0:T(4,128)} %add_convert_fusion) | copy-start | bytes 6148
  50.7 26.5 %collective-permute-start.5 = (bf16[4,96,1024]{2,1,0:T(8,128)(2,1)S(1)}, bf16[4,96,1024]{2,1,0:T(8,128)(2,1)S(1)}, u32[]{:S(2)}, u32[]{:S(2)}) collective-permute-start(bf16[4,96,1024]{2,1,0:T(8,128)(2,1)S(1)} %constant_dynamic-slice_fusion.refs_0_), channel_id=1, source_target_pairs={{0,2},{1,3},{2,0},{3,1},{4,6},{5,7},{6,4},{7,5},{8,10},{9,11},{10,... | collective-permute-start | bytes 2359304 | tf_op jit(solution)/shard_map/ppermute | solution.py:339
  52.3 26.5 %collective-permute-start.6 = (bf16[4,96,1024]{2,1,0:T(8,128)(2,1)S(1)}, bf16[4,96,1024]{2,1,0:T(8,128)(2,1)S(1)}, u32[]{:S(2)}, u32[]{:S(2)}) collective-permute-start(bf16[4,96,1024]{2,1,0:T(8,128)(2,1)S(1)} %constant_dynamic-slice_fusion.refs_0_), channel_id=1, source_target_pairs={{0,4},{1,5},{2,6},{3,7},{4,0},{5,1},{6,2},{7,3},{8,12},{9,13},{10,... | collective-permute-start | bytes 2359304 | tf_op jit(solution)/shard_map/ppermute | solution.py:339
  55.5 37.3 %copy-start.31 = (s32[4]{0:T(128)S(1)}, s32[4]{0:T(128)}, u32[]{:S(2)}) copy-start(s32[4]{0:T(128)} %compare_convert_fusion) | copy-start | bytes 52
  68.3 20.9 %collective-permute-start.9 = (bf16[2880,128]{1,0:T(8,128)(2,1)}, bf16[2880,128]{1,0:T(8,128)(2,1)S(1)}, u32[]{:S(2)}, u32[]{:S(2)}) collective-permute-start(bf16[2880,128]{1,0:T(8,128)(2,1)} %collective-permute-done.1.refs_2_), channel_id=1, source_target_pairs={{0,8},{1,9},{2,10},{3,11},{4,12},{5,13},{6,14},{7,15},{8,24},{9,25... | collective-permute-start | bytes 2211848 | tf_op jit(solution)/shard_map/ppermute | solution.py:332
  77.2 10.6 %collective-permute-start.7 = (bf16[2,96,1024]{2,1,0:T(8,128)(2,1)S(1)}, bf16[2,96,1024]{2,1,0:T(8,128)(2,1)}, u32[]{:S(2)}, u32[]{:S(2)}) collective-permute-start(bf16[2,96,1024]{2,1,0:T(8,128)(2,1)S(1)} %slice.60), channel_id=1, source_target_pairs={{0,4},{1,5},{2,6},{3,7},{4,0},{5,1},{6,2},{7,3},{8,12},{9,13},{10,... | collective-permute-start | bytes 1179656 | tf_op jit(solution)/shard_map/ppermute | solution.py:339
  78.8 10.4 %collective-permute-start.8 = (bf16[2,96,1024]{2,1,0:T(8,128)(2,1)S(1)}, bf16[2,96,1024]{2,1,0:T(8,128)(2,1)}, u32[]{:S(2)}, u32[]{:S(2)}) collective-permute-start(bf16[2,96,1024]{2,1,0:T(8,128)(2,1)S(1)} %slice.61), channel_id=1, source_target_pairs={{0,2},{1,3},{2,0},{3,1},{4,6},{5,7},{6,4},{7,5},{8,10},{9,11},{10,... | collective-permute-start | bytes 1179656 | tf_op jit(solution)/shard_map/ppermute | solution.py:339
  79.4 26.7 %collective-permute-start.11 = (bf16[4,96,1024]{2,1,0:T(8,128)(2,1)S(1)}, bf16[4,96,1024]{2,1,0:T(8,128)(2,1)S(1)}, u32[]{:S(2)}, u32[]{:S(2)}) collective-permute-start(bf16[4,96,1024]{2,1,0:T(8,128)(2,1)S(1)} %constant_dynamic-slice_fusion.refs_0_), channel_id=1, source_target_pairs={{0,1},{1,0},{2,3},{3,2},{4,5},{5,4},{6,7},{7,6},{8,9},{9,8},{10,11... | collective-permute-start | bytes 2359304 | tf_op jit(solution)/shard_map/ppermute | solution.py:339
  90.0 28.2 %collective-permute-start.12 = (bf16[4,96,1024]{2,1,0:T(8,128)(2,1)S(1)}, bf16[4,96,1024]{2,1,0:T(8,128)(2,1)}, u32[]{:S(2)}, u32[]{:S(2)}) collective-permute-start(bf16[4,96,1024]{2,1,0:T(8,128)(2,1)S(1)} %collective-permute-done.5.refs_2_), channel_id=1, source_target_pairs={{0,1},{1,0},{2,3},{3,2},{4,5},{5,4},{6,7},{7,6},{8,9},{9,8},{10,11... | collective-permute-start | bytes 2359304 | tf_op jit(solution)/shard_map/ppermute | solution.py:339
  90.0 28.2 %collective-permute-start.13 = (bf16[4,96,1024]{2,1,0:T(8,128)(2,1)S(1)}, bf16[4,96,1024]{2,1,0:T(8,128)(2,1)}, u32[]{:S(2)}, u32[]{:S(2)}) collective-permute-start(bf16[4,96,1024]{2,1,0:T(8,128)(2,1)S(1)} %collective-permute-done.6.refs_4_), channel_id=1, source_target_pairs={{0,1},{1,0},{2,3},{3,2},{4,5},{5,4},{6,7},{7,6},{8,9},{9,8},{10,11... | collective-permute-start | bytes 2359304 | tf_op jit(solution)/shard_map/ppermute | solution.py:339
  92.3 25.9 %collective-permute-start.14 = (bf16[2,96,1024]{2,1,0:T(8,128)(2,1)}, bf16[2,96,1024]{2,1,0:T(8,128)(2,1)}, u32[]{:S(2)}, u32[]{:S(2)}) collective-permute-start(bf16[2,96,1024]{2,1,0:T(8,128)(2,1)} %collective-permute-done.7.refs_6_), channel_id=1, source_target_pairs={{0,1},{1,0},{2,3},{3,2},{4,5},{5,4},{6,7},{7,6},{8,9},{9,8},{10,11... | collective-permute-start | bytes 1179656 | tf_op jit(solution)/shard_map/ppermute | solution.py:339
  92.3 25.9 %collective-permute-start.15 = (bf16[2,96,1024]{2,1,0:T(8,128)(2,1)}, bf16[2,96,1024]{2,1,0:T(8,128)(2,1)}, u32[]{:S(2)}, u32[]{:S(2)}) collective-permute-start(bf16[2,96,1024]{2,1,0:T(8,128)(2,1)} %collective-permute-done.8.refs_8_), channel_id=1, source_target_pairs={{0,1},{1,0},{2,3},{3,2},{4,5},{5,4},{6,7},{7,6},{8,9},{9,8},{10,11... | collective-permute-start | bytes 1179656 | tf_op jit(solution)/shard_map/ppermute | solution.py:339
  106.1 12.1 %collective-permute-start.10 = (bf16[4,128,256]{2,1,0:T(8,128)(2,1)S(1)}, bf16[4,128,256]{2,1,0:T(8,128)(2,1)S(1)}, u32[]{:S(2)}, u32[]{:S(2)}) collective-permute-start(bf16[4,128,256]{2,1,0:T(8,128)(2,1)S(1)} %get-tuple-element.40.key_values_ref), channel_id=1, source_target_pairs={{0,1},{1,2},{2,3},{3,4},{4,5},{5,6},{6,7},{7,0},{8,9},{9,10},{10,1... | collective-permute-start | bytes 786440 | tf_op jit(solution)/shard_map/ppermute | solution.py:336
  124.9 20.2 %collective-permute-start.16 = (bf16[2880,128]{1,0:T(8,128)(2,1)S(1)}, bf16[2880,128]{1,0:T(8,128)(2,1)S(1)}, u32[]{:S(2)}, u32[]{:S(2)}) collective-permute-start(bf16[2880,128]{1,0:T(8,128)(2,1)S(1)} %convert_bitcast_fusion), channel_id=1, source_target_pairs={{0,8},{1,9},{2,10},{3,11},{4,12},{5,13},{6,14},{7,15},{8,24},{9,25... | collective-permute-start | bytes 2211848 | tf_op jit(solution)/shard_map/ppermute | solution.py:332
  145.2 37.6 %copy-start.18 = (bf16[128,2880]{0,1:T(8,128)(2,1)S(1)}, bf16[128,2880]{0,1:T(8,128)(2,1)}, u32[]{:S(2)}) copy-start(bf16[128,2880]{0,1:T(8,128)(2,1)} %param.14) | copy-start | bytes 2211844
  145.2 19.1 %collective-permute-start.17 = (bf16[2880,128]{1,0:T(8,128)(2,1)S(1)}, bf16[2880,128]{1,0:T(8,128)(2,1)S(1)}, u32[]{:S(2)}, u32[]{:S(2)}) collective-permute-start(bf16[2880,128]{1,0:T(8,128)(2,1)S(1)} %fusion.12), channel_id=1, source_target_pairs={{0,8},{1,9},{2,10},{3,11},{4,12},{5,13},{6,14},{7,15},{8,24},{9,25... | collective-permute-start | bytes 2211848 | tf_op jit(solution)/shard_map/ppermute | solution.py:332
  164.5 19.5 %copy-start.26 = (f32[2880]{0:T(1024)S(1)}, f32[2880]{0:T(1024)}, u32[]{:S(2)}) copy-start(f32[2880]{0:T(1024)} %param.18) | copy-start | bytes 34564
  164.5 18.3 %collective-permute-start.18 = (bf16[2880,128]{1,0:T(8,128)(2,1)S(1)}, bf16[2880,128]{1,0:T(8,128)(2,1)S(1)}, u32[]{:S(2)}, u32[]{:S(2)}) collective-permute-start(bf16[2880,128]{1,0:T(8,128)(2,1)S(1)} %fusion.10), channel_id=1, source_target_pairs={{0,8},{1,9},{2,10},{3,11},{4,12},{5,13},{6,14},{7,15},{8,24},{9,25... | collective-permute-start | bytes 2211848 | tf_op jit(solution)/shard_map/ppermute | solution.py:332
  187.4 57.3 %all-to-all-start = ((bf16[32,3,4,2880]{3,2,1,0:T(4,128)(2,1)}), bf16[32,3,4,2880]{3,2,1,0:T(4,128)(2,1)}, u32[]{:S(2)}, u32[]{:S(2)}) async-start(bf16[32,3,4,2880]{3,2,1,0:T(4,128)(2,1)} %reshape.261), calls=%async_computation | async-start | bytes 4521984 | tf_op jit(solution)/shard_map/all_to_all | solution.py:523
  244.7 41.8 %all-to-all-start.1 = ((bf16[32,8,2880]{2,1,0:T(8,128)(2,1)}), bf16[32,8,2880]{2,1,0:T(8,128)(2,1)S(1)}, u32[]{:S(2)}, u32[]{:S(2)}) async-start(bf16[32,8,2880]{2,1,0:T(8,128)(2,1)} %bitcast.25), calls=%async_computation.1 | async-start | bytes 3014656 | tf_op jit(solution)/shard_map/all_to_all | solution.py:523
  287.6 58.6 %all-to-all-start.2 = ((bf16[32,3,4,2880]{3,2,1,0:T(4,128)(2,1)}), bf16[32,3,4,2880]{3,2,1,0:T(4,128)(2,1)S(1)}, u32[]{:S(2)}, u32[]{:S(2)}) async-start(bf16[32,3,4,2880]{3,2,1,0:T(4,128)(2,1)} %reshape.264), calls=%async_computation.2 | async-start | bytes 4521984 | tf_op jit(solution)/shard_map/all_to_all | solution.py:523
  346.2 40.5 %all-to-all-start.3 = ((bf16[32,8,2880]{2,1,0:T(8,128)(2,1)}), bf16[32,8,2880]{2,1,0:T(8,128)(2,1)}, u32[]{:S(2)}, u32[]{:S(2)}) async-start(bf16[32,8,2880]{2,1,0:T(8,128)(2,1)} %bitcast.29), calls=%async_computation.3 | async-start | bytes 3014656 | tf_op jit(solution)/shard_map/all_to_all | solution.py:523
  352.8 33.9 %copy-start.24 = (bf16[256,256]{1,0:T(8,128)(2,1)S(1)}, bf16[256,256]{1,0:T(8,128)(2,1)}, u32[]{:S(2)}) copy-start(bf16[256,256]{1,0:T(8,128)(2,1)} %fusion.21) | copy-start | bytes 393220
  (24 other events, 80.5 us)
Sparse Core Ops, SparseCore 0:
  9.2 60.2 all-gather.2

commit v2 on v1

--- a/solution.py
+++ b/solution.py
@@ -163,7 +163,7 @@
             pltpu.VMEM((2, planes, share, (packed - width) // (2 * share) * cols), BF16),
             pltpu.SemaphoreType.DMA,
         ],
-        compiler_params=pltpu.CompilerParams(vmem_limit_bytes=40 * 2**20),
+        compiler_params=pltpu.CompilerParams(vmem_limit_bytes=58 * 2**20),
         cost_estimate=pl.CostEstimate(
             flops=2 * count * rows * width * kv_cols,
             bytes_accessed=2 * width * (kv_cols + 2 * count * rows),
@@ -202,7 +202,7 @@
         out_specs=vmem,
         out_shape=jax.ShapeDtypeStruct((count, rows, planes * cols), BF16),
         scratch_shapes=[pltpu.VMEM((planes, width, cols), BF16), pltpu.SemaphoreType.DMA((planes // 2,))],
-        compiler_params=pltpu.CompilerParams(vmem_limit_bytes=40 * 2**20),
+        compiler_params=pltpu.CompilerParams(vmem_limit_bytes=58 * 2**20),
         cost_estimate=pl.CostEstimate(
             flops=2 * count * rows * width * planes * cols,
             bytes_accessed=2 * width * (planes * cols + count * rows),
@@ -410,12 +410,12 @@
     return (tokens_t.astype(F32) + total).astype(BF16), early
 
 
-def expert_kernel(tile, hidden, rows_ref, gate_ref, upper_ref, down_ref, out_ref, total_ref):
+def expert_kernel(tile, hidden, rows_ref, gate_ref, upper_ref, down_ref, out_ref, total_ref, flat_ref):
     step = pl.program_id(0)
     steps = pl.num_programs(0)
 
     def add(count, initial):
-        rows = rows_ref[...]
+        rows = flat_ref[...]
         gate = dot32(rows, gate_ref[0, :, :count])
         upper = dot32(rows, upper_ref[0, :, :count])
         activation = (gate * jax.nn.sigmoid(1.702 * gate) * (upper + 1.0)).astype(BF16)
@@ -426,6 +426,7 @@
 
     @pl.when(step == 0)
     def _():
+        flat_ref[...] = rows_ref[...].reshape(flat_ref.shape)
         add(tile, True)
 
     @pl.when(jnp.logical_and(step > 0, step < steps - 1))
@@ -435,25 +436,27 @@
     @pl.when(step == steps - 1)
     def _():
         add(last, False)
-        out_ref[...] = total_ref[...].astype(BF16)
+        out_ref[...] = total_ref[...].astype(BF16).reshape(out_ref.shape)
 
 
 def run_expert(rows, gate_up, down):
-    count, width = rows.shape
+    width = rows.shape[-1]
+    count = rows.size // width
     hidden = down.shape[0]
     tile = 512 if hidden > 1024 else 256
+    whole = pl.BlockSpec(rows.shape, lambda f: (0,) * rows.ndim)
     return pl.pallas_call(
         functools.partial(expert_kernel, tile, hidden),
         grid=(-(-hidden // tile),),
         in_specs=[
-            pl.BlockSpec((count, width), lambda f: (0, 0)),
+            whole,
             pl.BlockSpec((1, width, tile), lambda f: (0, 0, f)),
             pl.BlockSpec((1, width, tile), lambda f: (1, 0, f)),
             pl.BlockSpec((tile, width), lambda f: (f, 0)),
         ],
-        out_specs=pl.BlockSpec((count, width), lambda f: (0, 0)),
-        out_shape=jax.ShapeDtypeStruct((count, width), BF16),
-        scratch_shapes=[pltpu.VMEM((count, width), F32)],
+        out_specs=whole,
+        out_shape=jax.ShapeDtypeStruct(rows.shape, BF16),
+        scratch_shapes=[pltpu.VMEM((count, width), F32), pltpu.VMEM((count, width), BF16)],
         compiler_params=pltpu.CompilerParams(vmem_limit_bytes=52 * 2**20),
         cost_estimate=pl.CostEstimate(
             flops=6 * count * width * hidden,
@@ -468,15 +471,16 @@
 
 
 def dispatch_kernel(chosen_ref, normed_ref, out_ref):
-    out_ref[...] = dot_nt(chosen_ref[...], normed_ref[...]).astype(BF16)
-
-
-def dispatch(chosen, normed):
+    out_ref[...] = dot_nt(chosen_ref[...], normed_ref[...]).astype(BF16).reshape(out_ref.shape)
+
+
+def dispatch(chosen, normed, size):
     total, rows = chosen.shape
     width = normed.shape[0]
+    shape = (total // 4, 4, width) if size % 8 and size % 4 == 0 else (total, width)
     return pl.pallas_call(
         dispatch_kernel,
-        out_shape=jax.ShapeDtypeStruct((total, width), BF16),
+        out_shape=jax.ShapeDtypeStruct(shape, BF16),
         compiler_params=pltpu.CompilerParams(vmem_limit_bytes=24 * 2**20),
         cost_estimate=pl.CostEstimate(
             flops=2 * total * rows * width, bytes_accessed=2 * width * (total + rows), transcendentals=0
@@ -514,13 +518,9 @@
     n_ctx, n_exp = lax.axis_size("ctx"), lax.axis_size("exp")
     width_local = width // n_exp
 
-    def tiles(rows, size):
-        if size % 8 == 0 or size % 4:
-            return rows.reshape(n_ctx, size, -1)
-        return rows.reshape(n_ctx, size // 4, 4, -1)
-
     def exchange(parts):
-        return lax.all_to_all(parts, "ctx", split_axis=0, concat_axis=0, tiled=True)
+        by_device = parts.reshape((n_ctx, -1) + parts.shape[1:])
+        return lax.all_to_all(by_device, "ctx", split_axis=0, concat_axis=0, tiled=True)
 
     def in_order(parts, earlier):
         return lax.optimization_barrier((parts, earlier))
@@ -529,7 +529,7 @@
     for size, (chosen, _) in zip(sizes, matrices):
         if outgoing:
             chosen, outgoing[-1] = in_order(chosen, outgoing[-1])
-        outgoing.append(tiles(dispatch(chosen, normed), size))
+        outgoing.append(dispatch(chosen, normed, size))
     for parts in outgoing:
         if received:
             parts, received[-1] = in_order(parts, received[-1])
@@ -541,8 +541,8 @@
             received[i], results[0] = in_order(received[i], results[0])
         if results:
             received[i], results[-1] = in_order(received[i], results[-1])
-        rows_in = received[i].reshape(n_ctx * size, width)
-        results.append(tiles(run_expert(rows_in, gate_up, down), size))
+        rows_in = received[i].reshape(outgoing[i].shape)
+        results.append(run_expert(rows_in, gate_up, down))
 
     answers = []
     for parts in results:

time: 403 us -> 393 us (0.975)
  local copies, waits for them, and re-layouts: 32.8 us -> 11 us
  waiting for transfers between devices: 201 us -> 212 us
  Pallas kernels: 87.9 us -> 94.6 us
    unnamed x70 -> x52, local copies, waits for them, and re-layouts: 16 us -> 4.65 us
    reshape x3 -> x0, local copies, waits for them, and re-layouts: 10.5 us -> none  [the longest x2 6.18 us: tiles(): return rows.reshape(n_ctx, size // 4, 4, -1)]
    all_to_all x4, waiting for transfers between devices: 111 us -> 118 us  [exchange(): lax.all_to_all(by_device, 'ctx', split_axis=0, concat_axis=0, tiled=True)]
  transfers between devices with their start and end apart: 24 -> 24, of which waited for: 12 -> 13; matrix products, arithmetic and copies ran while one was open for 8% -> 5% of each run, Pallas kernels for 20% -> 22%
where the time goes in v2:
time: 393 us; the launch traced here: 387 us
  waiting for transfers between devices  212 us (54%)
  Pallas kernels  94.6 us (24%)
  starting transfers between devices  37.2 us (9%)
  between operations  14.3 us (4%)
  other arithmetic  12.9 us (3%)
  local copies, waits for them, and re-layouts  11 us (3%)
  matrix products  5.34 us (1%)
    all_to_all x4, waiting for transfers between devices, exchange(): lax.all_to_all(by_device, 'ctx', split_axis=0, concat_axis=0, tiled=True)  118 us
    ppermute x6, waiting for transfers between devices, pass_on(): return lax.ppermute(block, 'ctx', route)  68.8 us
    pallas_call x2, Pallas kernels, run_expert(): pl.pallas_call(functools.partial(expert_kernel, tile, hidden), grid=(-(-h...  52.6 us
    pallas_call x2, Pallas kernels, attend_and_project(): pl.pallas_call(functools.partial(attend_kernel, numbers, pieces), in_spec...  20.5 us
    all_to_all x4, starting transfers between devices, exchange(): lax.all_to_all(by_device, 'ctx', split_axis=0, concat_axis=0, tiled=True)  17 us
    ppermute x9, waiting for transfers between devices, swap(): return lax.ppermute(block, 'ctx', [(i, i ^ bits) for i in range(n_ctx)])  14.1 us
    pallas_call x1, Pallas kernels, project_queries(): pl.pallas_call(query_kernel, in_specs=[vmem, pl.BlockSpec(memory_space=pl...  12.3 us
    ppermute x3, waiting for transfers between devices, shift(): lax.ppermute(block, 'ctx', [(i, (i + steps * PLANE) % n_ctx) for i in ran...  10.6 us
  transfers between devices with their start and end apart: 24, of which 13 were waited for; matrix products, arithmetic and copies ran while one was open for 5% of the time, Pallas kernels for 22%

profile of v2, /device:TPU:0, one launch (start us, length us, event | category | flops | bytes accessed | tf_op | source)
XLA Modules:
  0.0 387.0 jit_solution(6970532675804435230)
XLA Ops:
  11.9 5.0 %collective-permute-start.2 = (bf16[96,1024]{1,0:T(8,128)(2,1)}, bf16[96,1024]{1,0:T(8,128)(2,1)S(1)}, u32[]{:S(2)}, u32[]{:S(2)}) collective-permute-start(bf16[96,1024]{1,0:T(8,128)(2,1)} %get-tuple-element.65), channel_id=1, source_target_pairs={{0,24},{1,25},{2,26},{3,27},{4,28},{5,29},{6,30},{7,31},{8,0},{9,1... | collective-permute-start | bytes 589832 | tf_op jit(solution)/shard_map/ppermute | solution.py:326
  18.0 2.5 collective-permute-start
  24.2 10.6 %collective-permute-done.3 = bf16[96,1024]{1,0:T(8,128)(2,1)S(1)} collective-permute-done((bf16[96,1024]{1,0:T(8,128)(2,1)}, bf16[96,1024]{1,0:T(8,128)(2,1)S(1)}, u32[]{:S(2)}, u32[]{:S(2)}) %collective-permute-start.3) | collective-permute-done | bytes 196640 | tf_op jit(solution)/shard_map/ppermute | solution.py:326
  34.9 14.9 %collective-permute-done.refs_1_ = bf16[2880,128]{1,0:T(8,128)(2,1)} collective-permute-done((bf16[2880,128]{1,0:T(8,128)(2,1)S(1)}, bf16[2880,128]{1,0:T(8,128)(2,1)}, u32[]{:S(2)}, u32[]{:S(2)}) %collective-permute-start) | collective-permute-done | bytes 737312 | tf_op jit(solution)/shard_map/ppermute | solution.py:332
  55.2 13.4 %collective-permute-done.1.refs_2_ = bf16[2880,128]{1,0:T(8,128)(2,1)} collective-permute-done((bf16[2880,128]{1,0:T(8,128)(2,1)}, bf16[2880,128]{1,0:T(8,128)(2,1)}, u32[]{:S(2)}, u32[]{:S(2)}) %collective-permute-start.1) | collective-permute-done | bytes 737312 | tf_op jit(solution)/shard_map/ppermute | solution.py:332
  70.9 6.2 %collective-permute-done.5.refs_2_ = bf16[4,96,1024]{2,1,0:T(8,128)(2,1)S(1)} collective-permute-done((bf16[4,96,1024]{2,1,0:T(8,128)(2,1)S(1)}, bf16[4,96,1024]{2,1,0:T(8,128)(2,1)S(1)}, u32[]{:S(2)}, u32[]{:S(2)}) %collective-permute-start.5) | collective-permute-done | bytes 786464 | tf_op jit(solution)/shard_map/ppermute | solution.py:339
  79.4 1.8 negate_select_fusion
  81.2 6.5 %collective-permute-done.7.refs_6_ = bf16[2,96,1024]{2,1,0:T(8,128)(2,1)S(1)} collective-permute-done((bf16[2,96,1024]{2,1,0:T(8,128)(2,1)S(1)}, bf16[2,96,1024]{2,1,0:T(8,128)(2,1)S(1)}, u32[]{:S(2)}, u32[]{:S(2)}) %collective-permute-start.7) | collective-permute-done | bytes 393248 | tf_op jit(solution)/shard_map/ppermute | solution.py:339
  89.6 1.7 fusion.18
  92.7 5.3 %shard_map.136 = (bf16[512,2880]{1,0:T(8,128)(2,1)}, bf16[4,128,256]{2,1,0:T(8,128)(2,1)}) custom-call(bf16[2880,128]{1,0:T(8,128)(2,1)} %copy-done.11, bf16[2880,128]{1,0:T(8,128)(2,1)} %collective-permute-done.refs_1_, bf16[2880,128]{1,0:T(8,128)(2,1)} %collective-permute-done.1.refs_2_, bf16[2880,128]{1,0:T(8,128)(2,1)} %copy-done.16, ...), custom_call_target="tpu_custom_call" | custom-call | flops 754974720 | bytes 7372800 | tf_op jit(solution)/shard_map/pallas_call | solution.py:153
  98.6 12.3 %shard_map.137.queries_ref = bf16[4,128,1024]{2,1,0:T(8,128)(2,1)} custom-call(bf16[512,2880]{1,0:T(8,128)(2,1)} %get-tuple-element.39.rows_ref, bf16[8,3616,128]{2,1,0:T(8,128)(2,1)} %bitcast.99, f32[4,128,128]{2,1,0:T(8,128)} %get-tuple-element.37.refs_5_.cos_ref, f32[4,128,128]{2,1,0:T(8,128)} %get-tuple-element.38.refs_6_.sin_ref), custom_call_target="tpu_custom_call" | custom-call | flops 3019898880 | bytes 8847360 | tf_op jit(solution)/shard_map/pallas_call | solution.py:199
  112.2 6.5 %shard_map.138 = f32[1,2880,128]{2,1,0:T(8,128)S(1)} custom-call(s32[16]{0:T(128)S(1)} %pad_add_fusion.place_ref, f32[16]{0:T(128)S(1)} %dynamic_slice.24.sinks_ref, bf16[4,128,1024]{2,1,0:T(8,128)(2,1)S(1)} %copy-done, bf16[4,128,256]{2,1,0:T(8,128)(2,1)S(1)} %copy-done.1, bf16[4,128,256]{2,1,0:T(8,128)(2,1)S(1)} %collective-permute-done.10.halos_ref, ...), custom_call_target="tpu_custom_call" | custom-call | flops 1023410176 | bytes 7372800 | tf_op jit(solution)/shard_map/pallas_call | solution.py:294
  118.7 1.7 collective-permute-start.16
  120.4 14.1 %shard_map.139 = f32[3,2880,128]{2,1,0:T(8,128)S(1)} custom-call(s32[16]{0:T(128)S(1)} %pad_add_fusion.place_ref, f32[16]{0:T(128)S(1)} %dynamic_slice.24.sinks_ref, bf16[4,128,1024]{2,1,0:T(8,128)(2,1)S(1)} %copy-done, bf16[4,128,256]{2,1,0:T(8,128)(2,1)S(1)} %copy-done.1, bf16[4,128,256]{2,1,0:T(8,128)(2,1)S(1)} %collective-permute-done.10.halos_ref, ...), custom_call_target="tpu_custom_call" | custom-call | flops 3070230528 | bytes 10321920 | tf_op jit(solution)/shard_map/pallas_call | solution.py:294
  134.5 4.4 %collective-permute-done.16 = bf16[2880,128]{1,0:T(8,128)(2,1)S(1)} collective-permute-done((bf16[2880,128]{1,0:T(8,128)(2,1)S(1)}, bf16[2880,128]{1,0:T(8,128)(2,1)S(1)}, u32[]{:S(2)}, u32[]{:S(2)}) %collective-permute-start.16) | collective-permute-done | bytes 737312 | tf_op jit(solution)/shard_map/ppermute | solution.py:332
  139.7 18.5 %collective-permute-done.17 = bf16[2880,128]{1,0:T(8,128)(2,1)S(1)} collective-permute-done((bf16[2880,128]{1,0:T(8,128)(2,1)S(1)}, bf16[2880,128]{1,0:T(8,128)(2,1)S(1)}, u32[]{:S(2)}, u32[]{:S(2)}) %collective-permute-start.17) | collective-permute-done | bytes 737312 | tf_op jit(solution)/shard_map/ppermute | solution.py:332
  159.1 17.7 %collective-permute-done.18 = bf16[2880,128]{1,0:T(8,128)(2,1)S(1)} collective-permute-done((bf16[2880,128]{1,0:T(8,128)(2,1)S(1)}, bf16[2880,128]{1,0:T(8,128)(2,1)S(1)}, u32[]{:S(2)}, u32[]{:S(2)}) %collective-permute-start.18) | collective-permute-done | bytes 737312 | tf_op jit(solution)/shard_map/ppermute | solution.py:332
  178.5 2.2 shard_map.140
  180.6 4.6 %all-to-all-start = ((bf16[32,3,4,2880]{3,2,1,0:T(4,128)(2,1)}), bf16[32,3,4,2880]{3,2,1,0:T(4,128)(2,1)S(1)}, u32[]{:S(2)}, u32[]{:S(2)}) async-start(bf16[32,3,4,2880]{3,2,1,0:T(4,128)(2,1)} %bitcast.25), calls=%async_computation | async-start | bytes 4521984 | tf_op jit(solution)/shard_map/all_to_all | solution.py:523
  185.3 1.7 shard_map.141
  187.0 50.7 %all-to-all-done = bf16[32,3,4,2880]{3,2,1,0:T(4,128)(2,1)S(1)} async-done(((bf16[32,3,4,2880]{3,2,1,0:T(4,128)(2,1)}), bf16[32,3,4,2880]{3,2,1,0:T(4,128)(2,1)S(1)}, u32[]{:S(2)}, u32[]{:S(2)}) %all-to-all-start) | async-done | bytes 2211872 | tf_op jit(solution)/shard_map/all_to_all | solution.py:523
  239.1 4.3 %all-to-all-start.1 = ((bf16[32,8,2880]{2,1,0:T(8,128)(2,1)}), bf16[32,8,2880]{2,1,0:T(8,128)(2,1)}, u32[]{:S(2)}, u32[]{:S(2)}) async-start(bf16[32,8,2880]{2,1,0:T(8,128)(2,1)} %bitcast.26), calls=%async_computation.1 | async-start | bytes 3014656 | tf_op jit(solution)/shard_map/all_to_all | solution.py:523
  243.5 29.2 %shard_map.142 = bf16[96,4,2880]{2,1,0:T(4,128)(2,1)} custom-call(bf16[96,4,2880]{2,1,0:T(4,128)(2,1)} %bitcast.100, bf16[2,2880,2880]{2,1,0:T(8,128)(2,1)} %bitcast.92, bf16[2,2880,2880]{2,1,0:T(8,128)(2,1)} %bitcast.93, bf16[2880,2880]{1,0:T(8,128)(2,1)} %bitcast.96), custom_call_target="tpu_custom_call" | custom-call | flops 19110297600 | bytes 54190080 | tf_op jit(solution)/shard_map/pallas_call | solution.py:448
  272.7 7.1 %all-to-all-done.1 = bf16[32,8,2880]{2,1,0:T(8,128)(2,1)} async-done(((bf16[32,8,2880]{2,1,0:T(8,128)(2,1)}), bf16[32,8,2880]{2,1,0:T(8,128)(2,1)}, u32[]{:S(2)}, u32[]{:S(2)}) %all-to-all-start.1) | async-done | bytes 1474592 | tf_op jit(solution)/shard_map/all_to_all | solution.py:523
  279.8 4.0 %all-to-all-start.2 = ((bf16[32,3,4,2880]{3,2,1,0:T(4,128)(2,1)}), bf16[32,3,4,2880]{3,2,1,0:T(4,128)(2,1)S(1)}, u32[]{:S(2)}, u32[]{:S(2)}) async-start(bf16[32,3,4,2880]{3,2,1,0:T(4,128)(2,1)} %bitcast.101), calls=%async_computation.2 | async-start | bytes 4521984 | tf_op jit(solution)/shard_map/all_to_all | solution.py:523
  283.8 23.4 %shard_map.143 = bf16[256,2880]{1,0:T(8,128)(2,1)} custom-call(bf16[256,2880]{1,0:T(8,128)(2,1)} %bitcast.30.rows_ref, bf16[2,2880,2880]{2,1,0:T(8,128)(2,1)} %bitcast.94, bf16[2,2880,2880]{2,1,0:T(8,128)(2,1)} %bitcast.95, bf16[2880,2880]{1,0:T(8,128)(2,1)} %bitcast.97), custom_call_target="tpu_custom_call" | custom-call | flops 12740198400 | bytes 52715520 | tf_op jit(solution)/shard_map/pallas_call | solution.py:448
  307.2 29.0 %all-to-all-done.2 = bf16[32,3,4,2880]{3,2,1,0:T(4,128)(2,1)S(1)} async-done(((bf16[32,3,4,2880]{3,2,1,0:T(4,128)(2,1)}), bf16[32,3,4,2880]{3,2,1,0:T(4,128)(2,1)S(1)}, u32[]{:S(2)}, u32[]{:S(2)}) %all-to-all-start.2) | async-done | bytes 2211872 | tf_op jit(solution)/shard_map/all_to_all | solution.py:523
  336.2 4.1 %all-to-all-start.3 = ((bf16[32,8,2880]{2,1,0:T(8,128)(2,1)}), bf16[32,8,2880]{2,1,0:T(8,128)(2,1)}, u32[]{:S(2)}, u32[]{:S(2)}) async-start(bf16[32,8,2880]{2,1,0:T(8,128)(2,1)} %bitcast.32), calls=%async_computation.3 | async-start | bytes 3014656 | tf_op jit(solution)/shard_map/all_to_all | solution.py:523
  340.3 2.5 reshape.266
  342.8 2.6 fusion.55
  345.4 31.2 %all-to-all-done.3 = bf16[32,8,2880]{2,1,0:T(8,128)(2,1)} async-done(((bf16[32,8,2880]{2,1,0:T(8,128)(2,1)}), bf16[32,8,2880]{2,1,0:T(8,128)(2,1)}, u32[]{:S(2)}, u32[]{:S(2)}) %all-to-all-start.3) | async-done | bytes 1474592 | tf_op jit(solution)/shard_map/all_to_all | solution.py:523
  376.7 2.0 fusion
  (131 shorter events, 30.9 us)
Async XLA Ops:
  6.5 86.1 %all-gather.3.cloned.1.call-start = ((), (), s32[]{:S(2)}) async-start(), calls=%async_computation.4 | async-start | bytes 8331264 | tf_op jit(solution)/shard_map/all_gather | solution.py:352
  11.0 11.5 %copy-start.21 = (s32[128,4]{0,1:T(4,128)S(1)}, s32[128,4]{0,1:T(4,128)}, u32[]{:S(2)}) copy-start(s32[128,4]{0,1:T(4,128)} %param.15) | copy-start | bytes 6148
  11.0 11.6 %copy-start.22 = (f32[128,4]{0,1:T(4,128)S(1)}, f32[128,4]{0,1:T(4,128)}, u32[]{:S(2)}) copy-start(f32[128,4]{0,1:T(4,128)} %param.16) | copy-start | bytes 6148
  11.9 12.2 %collective-permute-start.2 = (bf16[96,1024]{1,0:T(8,128)(2,1)}, bf16[96,1024]{1,0:T(8,128)(2,1)S(1)}, u32[]{:S(2)}, u32[]{:S(2)}) collective-permute-start(bf16[96,1024]{1,0:T(8,128)(2,1)} %get-tuple-element.65), channel_id=1, source_target_pairs={{0,24},{1,25},{2,26},{3,27},{4,28},{5,29},{6,30},{7,31},{8,0},{9,1... | collective-permute-start | bytes 589832 | tf_op jit(solution)/shard_map/ppermute | solution.py:326
  17.0 17.8 %collective-permute-start.3 = (bf16[96,1024]{1,0:T(8,128)(2,1)}, bf16[96,1024]{1,0:T(8,128)(2,1)S(1)}, u32[]{:S(2)}, u32[]{:S(2)}) collective-permute-start(bf16[96,1024]{1,0:T(8,128)(2,1)} %get-tuple-element.64), channel_id=1, source_target_pairs={{0,16},{1,17},{2,18},{3,19},{4,20},{5,21},{6,22},{7,23},{8,24},{9,... | collective-permute-start | bytes 589832 | tf_op jit(solution)/shard_map/ppermute | solution.py:326
  17.0 17.9 %collective-permute-start.4 = (bf16[96,1024]{1,0:T(8,128)(2,1)S(1)}, bf16[96,1024]{1,0:T(8,128)(2,1)S(1)}, u32[]{:S(2)}, u32[]{:S(2)}) collective-permute-start(bf16[96,1024]{1,0:T(8,128)(2,1)S(1)} %get-tuple-element.63), channel_id=1, source_target_pairs={{0,8},{1,9},{2,10},{3,11},{4,12},{5,13},{6,14},{7,15},{8,16},{9,17... | collective-permute-start | bytes 589832 | tf_op jit(solution)/shard_map/ppermute | solution.py:326
  18.0 31.8 %collective-permute-start = (bf16[2880,128]{1,0:T(8,128)(2,1)S(1)}, bf16[2880,128]{1,0:T(8,128)(2,1)}, u32[]{:S(2)}, u32[]{:S(2)}) collective-permute-start(bf16[2880,128]{1,0:T(8,128)(2,1)S(1)} %fusion.15.refs_0_), channel_id=1, source_target_pairs={{0,8},{1,9},{2,10},{3,11},{4,12},{5,13},{6,14},{7,15},{8,24},{9,25... | collective-permute-start | bytes 2211848 | tf_op jit(solution)/shard_map/ppermute | solution.py:332
  24.1 30.3 %copy-start.12 = (f32[384,384]{1,0:T(8,128)}, f32[384,384]{1,0:T(8,128)S(1)}, u32[]{:S(2)}) copy-start(f32[384,384]{1,0:T(8,128)S(1)} %fusion.22) | copy-start | bytes 1769476
  49.8 18.8 %collective-permute-start.1 = (bf16[2880,128]{1,0:T(8,128)(2,1)}, bf16[2880,128]{1,0:T(8,128)(2,1)}, u32[]{:S(2)}, u32[]{:S(2)}) collective-permute-start(bf16[2880,128]{1,0:T(8,128)(2,1)} %collective-permute-done.refs_1_), channel_id=1, source_target_pairs={{0,8},{1,9},{2,10},{3,11},{4,12},{5,13},{6,14},{7,15},{8,24},{9,25... | collective-permute-start | bytes 2211848 | tf_op jit(solution)/shard_map/ppermute | solution.py:332
  50.6 19.6 %copy-start.18 = (pred[256,128]{1,0:T(8,128)(4,1)S(1)}, pred[256,128]{1,0:T(8,128)(4,1)}, u32[]{:S(2)}) copy-start(pred[256,128]{1,0:T(8,128)(4,1)} %get-tuple-element.60) | copy-start | bytes 98308
  50.7 26.5 %collective-permute-start.5 = (bf16[4,96,1024]{2,1,0:T(8,128)(2,1)S(1)}, bf16[4,96,1024]{2,1,0:T(8,128)(2,1)S(1)}, u32[]{:S(2)}, u32[]{:S(2)}) collective-permute-start(bf16[4,96,1024]{2,1,0:T(8,128)(2,1)S(1)} %constant_dynamic-slice_fusion.refs_0_), channel_id=1, source_target_pairs={{0,2},{1,3},{2,0},{3,1},{4,6},{5,7},{6,4},{7,5},{8,10},{9,11},{10,... | collective-permute-start | bytes 2359304 | tf_op jit(solution)/shard_map/ppermute | solution.py:339
  52.2 26.5 %collective-permute-start.6 = (bf16[4,96,1024]{2,1,0:T(8,128)(2,1)S(1)}, bf16[4,96,1024]{2,1,0:T(8,128)(2,1)S(1)}, u32[]{:S(2)}, u32[]{:S(2)}) collective-permute-start(bf16[4,96,1024]{2,1,0:T(8,128)(2,1)S(1)} %constant_dynamic-slice_fusion.refs_0_), channel_id=1, source_target_pairs={{0,4},{1,5},{2,6},{3,7},{4,0},{5,1},{6,2},{7,3},{8,12},{9,13},{10,... | collective-permute-start | bytes 2359304 | tf_op jit(solution)/shard_map/ppermute | solution.py:339
  68.6 20.5 %collective-permute-start.9 = (bf16[2880,128]{1,0:T(8,128)(2,1)}, bf16[2880,128]{1,0:T(8,128)(2,1)S(1)}, u32[]{:S(2)}, u32[]{:S(2)}) collective-permute-start(bf16[2880,128]{1,0:T(8,128)(2,1)} %collective-permute-done.1.refs_2_), channel_id=1, source_target_pairs={{0,8},{1,9},{2,10},{3,11},{4,12},{5,13},{6,14},{7,15},{8,24},{9,25... | collective-permute-start | bytes 2211848 | tf_op jit(solution)/shard_map/ppermute | solution.py:332
  77.2 10.5 %collective-permute-start.7 = (bf16[2,96,1024]{2,1,0:T(8,128)(2,1)S(1)}, bf16[2,96,1024]{2,1,0:T(8,128)(2,1)S(1)}, u32[]{:S(2)}, u32[]{:S(2)}) collective-permute-start(bf16[2,96,1024]{2,1,0:T(8,128)(2,1)S(1)} %slice.60), channel_id=1, source_target_pairs={{0,4},{1,5},{2,6},{3,7},{4,0},{5,1},{6,2},{7,3},{8,12},{9,13},{10,... | collective-permute-start | bytes 1179656 | tf_op jit(solution)/shard_map/ppermute | solution.py:339
  78.7 10.4 %collective-permute-start.8 = (bf16[2,96,1024]{2,1,0:T(8,128)(2,1)S(1)}, bf16[2,96,1024]{2,1,0:T(8,128)(2,1)}, u32[]{:S(2)}, u32[]{:S(2)}) collective-permute-start(bf16[2,96,1024]{2,1,0:T(8,128)(2,1)S(1)} %slice.61), channel_id=1, source_target_pairs={{0,2},{1,3},{2,0},{3,1},{4,6},{5,7},{6,4},{7,5},{8,10},{9,11},{10,... | collective-permute-start | bytes 1179656 | tf_op jit(solution)/shard_map/ppermute | solution.py:339
  79.4 18.6 %collective-permute-start.11 = (bf16[4,96,1024]{2,1,0:T(8,128)(2,1)S(1)}, bf16[4,96,1024]{2,1,0:T(8,128)(2,1)S(1)}, u32[]{:S(2)}, u32[]{:S(2)}) collective-permute-start(bf16[4,96,1024]{2,1,0:T(8,128)(2,1)S(1)} %constant_dynamic-slice_fusion.refs_0_), channel_id=1, source_target_pairs={{0,1},{1,0},{2,3},{3,2},{4,5},{5,4},{6,7},{7,6},{8,9},{9,8},{10,11... | collective-permute-start | bytes 2359304 | tf_op jit(solution)/shard_map/ppermute | solution.py:339
  89.1 21.8 %collective-permute-start.12 = (bf16[4,96,1024]{2,1,0:T(8,128)(2,1)S(1)}, bf16[4,96,1024]{2,1,0:T(8,128)(2,1)}, u32[]{:S(2)}, u32[]{:S(2)}) collective-permute-start(bf16[4,96,1024]{2,1,0:T(8,128)(2,1)S(1)} %collective-permute-done.5.refs_2_), channel_id=1, source_target_pairs={{0,1},{1,0},{2,3},{3,2},{4,5},{5,4},{6,7},{7,6},{8,9},{9,8},{10,11... | collective-permute-start | bytes 2359304 | tf_op jit(solution)/shard_map/ppermute | solution.py:339
  89.1 21.8 %collective-permute-start.13 = (bf16[4,96,1024]{2,1,0:T(8,128)(2,1)S(1)}, bf16[4,96,1024]{2,1,0:T(8,128)(2,1)}, u32[]{:S(2)}, u32[]{:S(2)}) collective-permute-start(bf16[4,96,1024]{2,1,0:T(8,128)(2,1)S(1)} %collective-permute-done.6.refs_4_), channel_id=1, source_target_pairs={{0,1},{1,0},{2,3},{3,2},{4,5},{5,4},{6,7},{7,6},{8,9},{9,8},{10,11... | collective-permute-start | bytes 2359304 | tf_op jit(solution)/shard_map/ppermute | solution.py:339
  91.3 19.5 %collective-permute-start.14 = (bf16[2,96,1024]{2,1,0:T(8,128)(2,1)S(1)}, bf16[2,96,1024]{2,1,0:T(8,128)(2,1)}, u32[]{:S(2)}, u32[]{:S(2)}) collective-permute-start(bf16[2,96,1024]{2,1,0:T(8,128)(2,1)S(1)} %collective-permute-done.7.refs_6_), channel_id=1, source_target_pairs={{0,1},{1,0},{2,3},{3,2},{4,5},{5,4},{6,7},{7,6},{8,9},{9,8},{10,11... | collective-permute-start | bytes 1179656 | tf_op jit(solution)/shard_map/ppermute | solution.py:339
  91.4 19.5 %collective-permute-start.15 = (bf16[2,96,1024]{2,1,0:T(8,128)(2,1)}, bf16[2,96,1024]{2,1,0:T(8,128)(2,1)}, u32[]{:S(2)}, u32[]{:S(2)}) collective-permute-start(bf16[2,96,1024]{2,1,0:T(8,128)(2,1)} %collective-permute-done.8.refs_8_), channel_id=1, source_target_pairs={{0,1},{1,0},{2,3},{3,2},{4,5},{5,4},{6,7},{7,6},{8,9},{9,8},{10,11... | collective-permute-start | bytes 1179656 | tf_op jit(solution)/shard_map/ppermute | solution.py:339
  98.0 13.0 %collective-permute-start.10 = (bf16[4,128,256]{2,1,0:T(8,128)(2,1)}, bf16[4,128,256]{2,1,0:T(8,128)(2,1)S(1)}, u32[]{:S(2)}, u32[]{:S(2)}) collective-permute-start(bf16[4,128,256]{2,1,0:T(8,128)(2,1)} %get-tuple-element.40.key_values_ref), channel_id=1, source_target_pairs={{0,1},{1,2},{2,3},{3,4},{4,5},{5,6},{6,7},{7,0},{8,9},{9,10},{10,1... | collective-permute-start | bytes 786440 | tf_op jit(solution)/shard_map/ppermute | solution.py:336
  98.6 12.3 %copy-start.1 = (bf16[4,128,256]{2,1,0:T(8,128)(2,1)S(1)}, bf16[4,128,256]{2,1,0:T(8,128)(2,1)}, u32[]{:S(2)}) copy-start(bf16[4,128,256]{2,1,0:T(8,128)(2,1)} %get-tuple-element.40.key_values_ref) | copy-start | bytes 786436
  118.7 20.1 %collective-permute-start.16 = (bf16[2880,128]{1,0:T(8,128)(2,1)S(1)}, bf16[2880,128]{1,0:T(8,128)(2,1)S(1)}, u32[]{:S(2)}, u32[]{:S(2)}) collective-permute-start(bf16[2880,128]{1,0:T(8,128)(2,1)S(1)} %convert_bitcast_fusion), channel_id=1, source_target_pairs={{0,8},{1,9},{2,10},{3,11},{4,12},{5,13},{6,14},{7,15},{8,24},{9,25... | collective-permute-start | bytes 2211848 | tf_op jit(solution)/shard_map/ppermute | solution.py:332
  139.0 37.7 %copy-start.10 = (bf16[128,2880]{0,1:T(8,128)(2,1)S(1)}, bf16[128,2880]{0,1:T(8,128)(2,1)}, u32[]{:S(2)}) copy-start(bf16[128,2880]{0,1:T(8,128)(2,1)} %param.14) | copy-start | bytes 2211844
  139.0 19.2 %collective-permute-start.17 = (bf16[2880,128]{1,0:T(8,128)(2,1)S(1)}, bf16[2880,128]{1,0:T(8,128)(2,1)S(1)}, u32[]{:S(2)}, u32[]{:S(2)}) collective-permute-start(bf16[2880,128]{1,0:T(8,128)(2,1)S(1)} %fusion.12), channel_id=1, source_target_pairs={{0,8},{1,9},{2,10},{3,11},{4,12},{5,13},{6,14},{7,15},{8,24},{9,25... | collective-permute-start | bytes 2211848 | tf_op jit(solution)/shard_map/ppermute | solution.py:332
  158.4 19.6 %copy-start.20 = (f32[2880]{0:T(1024)S(1)}, f32[2880]{0:T(1024)}, u32[]{:S(2)}) copy-start(f32[2880]{0:T(1024)} %param.18) | copy-start | bytes 34564
  158.4 18.3 %collective-permute-start.18 = (bf16[2880,128]{1,0:T(8,128)(2,1)S(1)}, bf16[2880,128]{1,0:T(8,128)(2,1)S(1)}, u32[]{:S(2)}, u32[]{:S(2)}) collective-permute-start(bf16[2880,128]{1,0:T(8,128)(2,1)S(1)} %fusion.10), channel_id=1, source_target_pairs={{0,8},{1,9},{2,10},{3,11},{4,12},{5,13},{6,14},{7,15},{8,24},{9,25... | collective-permute-start | bytes 2211848 | tf_op jit(solution)/shard_map/ppermute | solution.py:332
  180.6 57.1 %all-to-all-start = ((bf16[32,3,4,2880]{3,2,1,0:T(4,128)(2,1)}), bf16[32,3,4,2880]{3,2,1,0:T(4,128)(2,1)S(1)}, u32[]{:S(2)}, u32[]{:S(2)}) async-start(bf16[32,3,4,2880]{3,2,1,0:T(4,128)(2,1)} %bitcast.25), calls=%async_computation | async-start | bytes 4521984 | tf_op jit(solution)/shard_map/all_to_all | solution.py:523
  239.1 40.7 %all-to-all-start.1 = ((bf16[32,8,2880]{2,1,0:T(8,128)(2,1)}), bf16[32,8,2880]{2,1,0:T(8,128)(2,1)}, u32[]{:S(2)}, u32[]{:S(2)}) async-start(bf16[32,8,2880]{2,1,0:T(8,128)(2,1)} %bitcast.26), calls=%async_computation.1 | async-start | bytes 3014656 | tf_op jit(solution)/shard_map/all_to_all | solution.py:523
  279.8 56.4 %all-to-all-start.2 = ((bf16[32,3,4,2880]{3,2,1,0:T(4,128)(2,1)}), bf16[32,3,4,2880]{3,2,1,0:T(4,128)(2,1)S(1)}, u32[]{:S(2)}, u32[]{:S(2)}) async-start(bf16[32,3,4,2880]{3,2,1,0:T(4,128)(2,1)} %bitcast.101), calls=%async_computation.2 | async-start | bytes 4521984 | tf_op jit(solution)/shard_map/all_to_all | solution.py:523
  336.2 40.5 %all-to-all-start.3 = ((bf16[32,8,2880]{2,1,0:T(8,128)(2,1)}), bf16[32,8,2880]{2,1,0:T(8,128)(2,1)}, u32[]{:S(2)}, u32[]{:S(2)}) async-start(bf16[32,8,2880]{2,1,0:T(8,128)(2,1)} %bitcast.32), calls=%async_computation.3 | async-start | bytes 3014656 | tf_op jit(solution)/shard_map/all_to_all | solution.py:523
  342.8 33.9 %copy-start.17 = (bf16[256,256]{1,0:T(8,128)(2,1)S(1)}, bf16[256,256]{1,0:T(8,128)(2,1)}, u32[]{:S(2)}) copy-start(bf16[256,256]{1,0:T(8,128)(2,1)} %fusion.21) | copy-start | bytes 393220
  (15 other events, 49.3 us)
Sparse Core Ops, SparseCore 0:
  9.2 60.1 all-gather.2
